TPU v7x, 256 devices: a whole 4x4x8 slice. The times are simulated.
256 devices in a mesh: rows: 16 (over y, x), vocab: 16 (over z, core).
Axes of the slice: x: 4, y: 4, z: 8, core: 2. Of those that a mesh axis runs over, the one named last changes fastest.
Arguments:
- hidden: bfloat16 [16, 1024, 4096], P('rows', None, 'vocab'), may hold values from -1024 to 1024
- mask_positions: int32 [16, 1024], P('rows'), may hold values from 0 to 1023, each once within a row
- counts: int32 [16], replicated, may hold values from 1 to 64, 512 in all
- targets: int32 [16, 1024], P('rows'), may hold values from 0 to 126463
- mask_ratio: int32 [16], P('rows'), may hold values from 1 to 16
- out_weight: bfloat16 [4096, 126464], P(None, ('rows', 'vocab')), may hold values from -1 to 1
Outputs:
- grad_hidden: float32 [16, 1024, 4096], P('rows', None, 'vocab')
Inputs may be any that keep to these rules, and one draw needn't show every extreme that they name: counts sum to 512; some sequence has exactly 64. The first counts[s] entries of row s of mask_positions are its masked positions.
All inputs are finite; a program needn't handle non-finite values.
Results may differ from a plain program's by a relative error of at most 0.0022.
Values may be sent and summed in bfloat16 or wider, within the bound.
No kernel may reach another device: no remote copies, remote signals or barrier semaphores. Data moves between devices by JAX's collectives and lax.ppermute only.
A program may use at most 64 MiB of HBM per device.

v0:
```python
import functools

import jax
import jax.numpy as jnp
from jax import lax
from jax.experimental import pallas as pl
from jax.experimental.pallas import tpu as pltpu
from jax.sharding import Mesh
from jax.sharding import PartitionSpec as P

weight_scale = 4.0
SIDE = 4
DEEP = 8
SEQS = SIDE * SIDE
SLOTS = 32
ROWS = 256
CHUNK = ROWS // 2
AUX = 128
PLANE = ("y", "x")
CHIPS = ("y", "x", "z")
NT = (((1,), (1,)), ((), ()))
TN = (((0,), (0,)), ((), ()))
SENT_SCALE = 4096.0


def chip_index():
    return lax.axis_index("y") * SIDE + lax.axis_index("x")


def first_row(start, core):
    return start + ((start + core) & 1)


def own_rows(counts_ref, ratio_ref, positions_ref, targets_ref, hidden_ref, keep_ref, aux_ref, give_ref, places_ref):
    seq = chip_index()
    core = lax.axis_index("c")
    start = jnp.int32(0)
    count = jnp.int32(0)
    for i in range(SEQS):
        start = start + jnp.where(i < seq, counts_ref[i], 0)
        count = count + jnp.where(i == seq, counts_ref[i], 0)
    length = hidden_ref.shape[0]
    q = lax.broadcasted_iota(jnp.int32, (2 * SLOTS, 1), 0)
    index = jnp.where(q < SLOTS, first_row(start, core), first_row(start, 1 - core)) - start + 2 * (q & (SLOTS - 1))
    valid = index < count
    at = lax.broadcasted_iota(jnp.int32, (2 * SLOTS, 128), 1)
    near = jnp.where(at == index, positions_ref[:, :128].astype(jnp.float32), 0.0)
    places = jnp.where(valid, jnp.sum(near, axis=1, keepdims=True), -1.0)
    places_ref[...] = jnp.transpose(jnp.broadcast_to(places, (2 * SLOTS, 128)))[:8].astype(jnp.int32)
    at = lax.broadcasted_iota(jnp.int32, (2 * SLOTS, length), 1)
    hit = at == places.astype(jnp.int32)
    rows = jnp.dot(jnp.where(hit, 1.0, 0.0).astype(jnp.bfloat16), hidden_ref[...], preferred_element_type=jnp.float32)
    rows = rows.astype(jnp.bfloat16)
    target = jnp.sum(jnp.where(hit, targets_ref[...].astype(jnp.float32), 0.0), axis=1, keepdims=True).astype(jnp.int32)
    lane = lax.broadcasted_iota(jnp.int32, (SLOTS, AUX), 1)
    own = target[:SLOTS]
    digits = jnp.where(lane == 0, own & 127, 0)
    digits = jnp.where(lane == 1, (own >> 7) & 127, digits)
    digits = jnp.where(lane == 2, own >> 14, digits)
    digits = jnp.where(lane == 3, ratio_ref[0], digits)
    keep_ref[...] = rows[:SLOTS]
    aux_ref[...] = digits.astype(jnp.float32).astype(jnp.bfloat16)
    give_ref[...] = rows[SLOTS:]


def slot_dest(counts_ref, slot_index, core):
    slot = slot_index & (SLOTS - 1)
    dest = jnp.full_like(slot_index, -1)
    start = jnp.int32(0)
    for i in range(SEQS):
        end = start + counts_ref[i]
        first = first_row(start, core)
        mine = ((slot_index >> 5) == i) & (first + 2 * slot < end)
        dest = jnp.where(mine, (first >> 1) + slot, dest)
        start = end
    return dest


def pack_rows(counts_ref, slots_ref, low_ref, high_ref, row_ref):
    core = lax.axis_index("c")
    dest = slot_dest(counts_ref, lax.broadcasted_iota(jnp.int32, (1, SEQS * SLOTS), 1), core)
    at = lax.broadcasted_iota(jnp.int32, (ROWS, SEQS * SLOTS), 0)
    pick = jnp.where(at == dest, 1.0, 0.0).astype(jnp.bfloat16)
    packed = jnp.dot(pick, slots_ref[...], preferred_element_type=jnp.float32)
    feat = (slots_ref.shape[1] - AUX) // 2
    own, near = packed[:, :feat], packed[:, feat:2 * feat]
    for at, part in ((0, jnp.where(core == 0, own, near)), (feat, jnp.where(core == 0, near, own))):
        part = part.astype(jnp.bfloat16)
        low_ref[:, at:at + feat] = part[:CHUNK]
        high_ref[:, at:at + feat] = part[CHUNK:]
    digits = jnp.transpose(packed[:, 2 * feat:])
    row_ref[0:1] = digits[0:1] + 128.0 * digits[1:2] + 16384.0 * digits[2:3]
    row_ref[1:2] = weight_scale / digits[3:4]


def features_of(away, span):
    return pl.ds(pl.multiple_of(((lax.axis_index("z") + away) & (DEEP - 1)) * span, span), span)


def score_rows(own_ref, near_ref, *refs):
    chunks, (own_scores_ref, near_scores_ref, stats_ref, rows) = refs[:2 * DEEP], refs[2 * DEEP:]
    count = own_ref.shape[0]
    for away in range(DEEP):
        features = features_of(away, chunks[0].shape[1])
        rows[:CHUNK, features] = chunks[2 * away][...]
        rows[CHUNK:, features] = chunks[2 * away + 1][...]
    for w_ref, ref in ((own_ref, own_scores_ref), (near_ref, near_scores_ref)):
        ref[:count] = lax.dot_general(w_ref[...], rows[...], NT, preferred_element_type=jnp.float32)
    at = lax.broadcasted_iota(jnp.int32, own_scores_ref.shape, 0)
    parts = [jnp.where(at < count, ref[...], -jnp.inf) for ref in (own_scores_ref, near_scores_ref)]
    own_scores_ref[...], near_scores_ref[...] = parts
    top = jnp.maximum(*[jnp.max(part, axis=0, keepdims=True) for part in parts])
    total = sum(jnp.sum(jnp.exp(part - top), axis=0, keepdims=True) for part in parts)
    stats = jnp.concatenate([top, total], axis=0)
    stats_ref[...] = jnp.broadcast_to(stats[None], stats_ref.shape)


def grad_rows(aways, own_slope_ref, near_slope_ref, own_ref, near_ref, *sums_refs):
    count = own_ref.shape[0]
    for i, away in enumerate(aways):
        features = features_of(away, sums_refs[0].shape[1])
        sums = jnp.dot(own_slope_ref[:, :count], own_ref[:, features], preferred_element_type=jnp.float32)
        sums += jnp.dot(near_slope_ref[:, :count], near_ref[:, features], preferred_element_type=jnp.float32)
        sums = sums * SENT_SCALE
        sums_refs[2 * i][...] = sums[:CHUNK]
        sums_refs[2 * i + 1][...] = sums[CHUNK:]


def slope_rows(aways, stats_ref, row_ref, own_scores_ref, near_scores_ref, own_ref, near_ref, own_slope_ref, near_slope_ref, *sums_refs):
    count = own_ref.shape[0]
    tops = stats_ref[:, 0, :]
    top = jnp.max(tops, axis=0, keepdims=True)
    total = jnp.sum(stats_ref[:, 1, :] * jnp.exp(tops - top), axis=0, keepdims=True)
    chip = chip_index() * DEEP + lax.axis_index("z")
    core = lax.axis_index("c")
    target = row_ref[0:1].astype(jnp.int32)
    at = lax.broadcasted_iota(jnp.int32, own_scores_ref.shape, 0)
    for ref, slope, of_core in ((own_scores_ref, own_slope_ref, core), (near_scores_ref, near_slope_ref, 1 - core)):
        local_target = target - (chip * 2 + of_core) * count
        probs = jnp.exp(ref[...] - top) / total
        onehot = jnp.where((at == local_target) & (at < count), 1.0, 0.0)
        slope[...] = jnp.transpose(row_ref[1:2] * (probs - onehot)).astype(jnp.bfloat16)
    grad_rows(aways, own_slope_ref, near_slope_ref, own_ref, near_ref, *sums_refs)


def spread_rows(counts_ref, low_ref, high_ref, slots_ref):
    dest = slot_dest(counts_ref, lax.broadcasted_iota(jnp.int32, (1, SEQS * SLOTS), 1), lax.axis_index("c"))
    at = lax.broadcasted_iota(jnp.int32, (ROWS, SEQS * SLOTS), 0)
    pick = jnp.where(at == dest, 1.0, 0.0).astype(jnp.bfloat16)
    rest = jnp.concatenate([low_ref[...], high_ref[...]], axis=0)
    part = rest.astype(jnp.bfloat16)
    rest = (rest - part.astype(jnp.float32)).astype(jnp.bfloat16)
    slots = lax.dot_general(pick, part, TN, preferred_element_type=jnp.float32)
    slots_ref[...] = slots + lax.dot_general(pick, rest, TN, preferred_element_type=jnp.float32)


def place_rows(places_ref, kept_ref, got_ref, out_ref):
    length = out_ref.shape[0]
    at = lax.broadcasted_iota(jnp.int32, (length, 2 * SLOTS), 0)
    hit = jnp.where(at == places_ref[0:1], 1.0, 0.0).astype(jnp.bfloat16)
    rest = jnp.concatenate([kept_ref[...], got_ref[...]], axis=0)
    out = None
    for _ in range(3):
        part = rest.astype(jnp.bfloat16)
        rest = rest - part.astype(jnp.float32)
        part = jnp.dot(hit, part, preferred_element_type=jnp.float32)
        out = part if out is None else out + part
    out_ref[...] = out


def swap_cores(x):
    return lax.ppermute(x, "c", [(0, 1), (1, 0)])


def pass_on(x, by):
    return lax.ppermute(x, "z", [(i, (i + by) % DEEP) for i in range(DEEP)])


def gather_chips(low, high):
    lows, highs = {0: low}, {0: high}
    for hop in range(1, DEEP // 2 + 1):
        lows[-hop] = pass_on(lows[1 - hop], 1)
        highs[hop] = pass_on(highs[hop - 1], -1)
        if hop < DEEP // 2:
            highs[-hop] = pass_on(highs[1 - hop], 1)
            lows[hop] = pass_on(lows[hop - 1], -1)
    lows[DEEP // 2] = lows[-(DEEP // 2)]
    return [chunk for away in range(DEEP) for chunk in (lows[(away + 3) % DEEP - 3], highs[(away + 3) % DEEP - 3])]


def reduce_chips(lows, highs):
    def send(x, by):
        return pass_on(x.astype(jnp.float16), by).astype(jnp.float32)

    half = DEEP // 2
    low_right, high_left = lows[half], highs[half]
    low_left, high_right = lows[half + 1], highs[half - 1]
    for hop in range(1, half):
        low_right = send(low_right, 1) + lows[half - hop]
        high_left = send(high_left, -1) + highs[half + hop]
        if hop < half - 1:
            low_left = send(low_left, -1) + lows[half + 1 + hop]
            high_right = send(high_right, 1) + highs[half - 1 - hop]
    low = lows[0] + send(low_left, -1) + send(low_right, 1)
    high = highs[0] + send(high_right, 1) + send(high_left, -1)
    return low, high


def local(hidden, mask_positions, counts, targets, mask_ratio, own_weight):
    c = lax.axis_index("c")
    features, vocab_dev = own_weight.shape
    wide = -(-vocab_dev // 128) * 128
    length, feat = hidden.shape[1:]
    span = 2 * feat
    smem = pl.BlockSpec(memory_space=pltpu.SMEM)
    vmem = pl.BlockSpec(memory_space=pltpu.VMEM)
    params = pltpu.CompilerParams(vmem_limit_bytes=16 << 20)
    small = pltpu.CompilerParams(vmem_limit_bytes=8 << 20)
    shape = jax.ShapeDtypeStruct

    keep, aux, give, places = pl.pallas_call(
        own_rows,
        out_shape=(
            shape((SLOTS, feat), jnp.bfloat16),
            shape((SLOTS, AUX), jnp.bfloat16),
            shape((SLOTS, feat), jnp.bfloat16),
            shape((8, 2 * SLOTS), jnp.int32),
        ),
        in_specs=[smem, smem, vmem, vmem, vmem],
        out_specs=(vmem,) * 4,
        compiler_params=pltpu.CompilerParams(vmem_limit_bytes=56 << 20),
    )(counts, mask_ratio, mask_positions, targets, hidden[0])
    got = swap_cores(give)

    slots = jnp.concatenate([keep, got, aux], axis=1)
    give, own_weight = lax.optimization_barrier((give, own_weight))
    held = jnp.where(counts[0] > 0, own_weight, 0)
    slots, held = lax.optimization_barrier((slots, held))
    own_t, near_t = held.T, swap_cores(held).T
    slots = lax.all_to_all(jnp.broadcast_to(slots[None], (SEQS,) + slots.shape), PLANE, 0, 0, tiled=True)
    low, high, row_data = pl.pallas_call(
        pack_rows,
        out_shape=(
            shape((CHUNK, span), jnp.bfloat16),
            shape((CHUNK, span), jnp.bfloat16),
            shape((2, ROWS), jnp.float32),
        ),
        in_specs=[smem, vmem],
        out_specs=(vmem,) * 3,
        compiler_params=small,
    )(counts, slots.reshape(SEQS * SLOTS, span + AUX))

    chunks = gather_chips(low, high)
    own_scores, near_scores, stats = pl.pallas_call(
        score_rows,
        out_shape=(
            shape((wide, ROWS), jnp.float32),
            shape((wide, ROWS), jnp.float32),
            shape((SEQS * DEEP, 2, ROWS), jnp.float32),
        ),
        in_specs=[vmem] * (2 + 2 * DEEP),
        out_specs=(vmem,) * 3,
        scratch_shapes=[pltpu.VMEM((ROWS, DEEP * span), jnp.bfloat16)],
        compiler_params=params,
    )(own_t, near_t, *chunks)

    stats = lax.all_to_all(stats, CHIPS, 0, 0, tiled=True)
    parts = (4, 5, 3), (6, 2, 7, 1, 0)
    sums_shape = shape((CHUNK, span), jnp.float32)
    slope_shape = shape((ROWS, wide), jnp.bfloat16)
    own_slope, near_slope, *sums = pl.pallas_call(
        functools.partial(slope_rows, parts[0]),
        out_shape=(slope_shape, slope_shape) + (sums_shape,) * (2 * len(parts[0])),
        in_specs=[vmem] * 6,
        out_specs=(vmem,) * (2 + 2 * len(parts[0])),
        compiler_params=params,
    )(stats, row_data, own_scores, near_scores, own_t, near_t)
    more = pl.pallas_call(
        functools.partial(grad_rows, parts[1]),
        out_shape=(sums_shape,) * (2 * len(parts[1])),
        in_specs=[vmem] * 4,
        out_specs=(vmem,) * (2 * len(parts[1])),
        compiler_params=params,
    )(own_slope, near_slope, own_t, near_t)
    sums = lax.optimization_barrier((*sums, *more))
    lows = dict(zip(parts[0] + parts[1], sums[::2]))
    highs = dict(zip(parts[0] + parts[1], sums[1::2]))

    low, high = reduce_chips(lows, highs)
    back = pl.pallas_call(
        spread_rows,
        out_shape=shape((SEQS * SLOTS, span), jnp.float32),
        in_specs=[smem, vmem, vmem],
        out_specs=vmem,
        compiler_params=small,
    )(counts, low, high)
    back = back.astype(jnp.float16).reshape(SEQS, SLOTS, span)
    back, first_core = lax.optimization_barrier((back, c == 0))
    back = lax.all_to_all(back, PLANE, 0, 0, tiled=True)
    back = jnp.sum(back.astype(jnp.float32), axis=0) * (1.0 / SENT_SCALE)
    kept = jnp.where(first_core, back[:, :feat], back[:, feat:])
    given = jnp.where(first_core, back[:, feat:], back[:, :feat])
    grad = pl.pallas_call(
        place_rows,
        out_shape=shape((length, feat), jnp.float32),
        in_specs=[vmem] * 3,
        out_specs=vmem,
        compiler_params=small,
    )(places, kept, swap_cores(given))
    return grad[None]


def solution(mesh):
    fine = Mesh(mesh.devices.reshape(SIDE, SIDE, DEEP, 2), CHIPS + ("c",))
    vocab = ("z", "c")
    return jax.shard_map(
        local,
        mesh=fine,
        in_specs=(
            P(PLANE, None, vocab),
            P(PLANE, None),
            P(),
            P(PLANE, None),
            P(PLANE),
            P(None, CHIPS + ("c",)),
        ),
        out_specs=P(PLANE, None, vocab),
        check_vma=False,
    )
```

profile of v0, /device:TPU:1, one launch (start us, length us, event | category | flops | bytes accessed | tf_op | source)
XLA Modules:
  0.0 135.0 jit_solution(8980980487018625348)
XLA Ops:
  0.7 2.0 %shard_map.64 = (bf16[32,256]{1,0:T(8,128)(2,1)}, bf16[32,128]{1,0:T(8,128)(2,1)}, bf16[32,256]{1,0:T(8,128)(2,1)}, s32[8,64]{1,0:T(8,128)}) custom-call(s32[16]{0:T(128)} %counts_ref.5, s32[1]{0:T(128)S(6)} %copy.7.ratio_ref, s32[1,1024]{1,0:T(1,128)} %positions_ref.1, s32[1,1024]{1,0:T(1,128)} %targets_ref.1, bf16[1024,256]{1,0:T(8,128)(2,1)} %bitcast.17), custom_call_target="tpu_custom_call" | custom-call | tf_op jit(solution)/shard_map/pallas_call | solution.py:221
  2.6 3.2 %collective-permute-start = (bf16[32,256]{1,0:T(8,128)(2,1)}, bf16[32,256]{1,0:T(8,128)(2,1)S(1)}, u32[]{:S(2)}, u32[]{:S(2)}) collective-permute-start(bf16[32,256]{1,0:T(8,128)(2,1)} %get-tuple-element.56), channel_id=1, source_target_pairs={{0,1},{1,0},{2,3},{3,2},{4,5},{5,4},{6,7},{7,6},{8,9},{9,8},{10,11... | collective-permute-start | bytes 49160 | tf_op jit(solution)/shard_map/ppermute | solution.py:172
  6.5 0.0 copy-start.4
  6.6 2.4 %broadcast_select_fusion = bf16[4096,494]{0,1:T(8,128)(2,1)S(1)} fusion(bf16[4096,494]{0,1:T(8,128)(2,1)} %param.11, pred[]{:T(512)} %bitcast.1), kind=kLoop, calls=%fused_computation | loop fusion | flops 2023424 | bytes 8093697 | tf_op jit(solution)/shard_map/jit(_where)/select_n | solution.py:237
  9.0 0.1 collective-permute-start.1
  9.1 0.1 broadcast_in_dim.14
  9.2 16.8 %all_to_all.15 = bf16[16,32,640]{2,1,0:T(8,128)(2,1)S(1)} all-to-all(bf16[16,32,640]{2,1,0:T(8,128)(2,1)S(1)} %broadcast_in_dim.14), channel_id=1, replica_groups=mesh['y'=4,'x'=4,'z'=8,'c'=2] {'y','x'}, dimensions={0} | all-to-all | bytes 1310720 | tf_op jit(solution)/shard_map/all_to_all | solution.py:240
  26.0 1.0 shard_map.65
  27.0 1.7 %collective-permute-start.8 = (bf16[128,512]{1,0:T(8,128)(2,1)S(1)}, bf16[128,512]{1,0:T(8,128)(2,1)S(1)}, u32[]{:S(2)}, u32[]{:S(2)}) collective-permute-start(bf16[128,512]{1,0:T(8,128)(2,1)S(1)} %get-tuple-element.61.refs_0_), channel_id=1, source_target_pairs={{0,2},{2,4},{4,6},{6,8},{8,10},{10,12},{12,14},{14,0},{1,3},{3,5},... | collective-permute-start | bytes 393224 | tf_op jit(solution)/shard_map/ppermute | solution.py:176
  28.7 4.0 %collective-permute-start.3 = (bf16[128,512]{1,0:T(8,128)(2,1)S(1)}, bf16[128,512]{1,0:T(8,128)(2,1)S(1)}, u32[]{:S(2)}, u32[]{:S(2)}) collective-permute-start(bf16[128,512]{1,0:T(8,128)(2,1)S(1)} %get-tuple-element.62.refs_1_), channel_id=1, source_target_pairs={{0,14},{2,0},{4,2},{6,4},{8,6},{10,8},{12,10},{14,12},{1,15},{3,1}... | collective-permute-start | bytes 393224 | tf_op jit(solution)/shard_map/ppermute | solution.py:176
  32.7 1.4 %collective-permute-start.2 = (bf16[128,512]{1,0:T(8,128)(2,1)S(1)}, bf16[128,512]{1,0:T(8,128)(2,1)S(1)}, u32[]{:S(2)}, u32[]{:S(2)}) collective-permute-start(bf16[128,512]{1,0:T(8,128)(2,1)S(1)} %get-tuple-element.61.refs_0_), channel_id=1, source_target_pairs={{0,14},{2,0},{4,2},{6,4},{8,6},{10,8},{12,10},{14,12},{1,15},{3,1}... | collective-permute-start | bytes 393224 | tf_op jit(solution)/shard_map/ppermute | solution.py:176
  34.1 0.1 collective-permute-start.13
  34.2 0.8 collective-permute-done.8.refs_14_
  35.0 0.0 collective-permute-start.9
  35.0 0.0 collective-permute-done.3.refs_3_
  35.0 2.8 %collective-permute-start.5 = (bf16[128,512]{1,0:T(8,128)(2,1)S(1)}, bf16[128,512]{1,0:T(8,128)(2,1)S(1)}, u32[]{:S(2)}, u32[]{:S(2)}) collective-permute-start(bf16[128,512]{1,0:T(8,128)(2,1)S(1)} %collective-permute-done.3.refs_3_), channel_id=1, source_target_pairs={{0,14},{2,0},{4,2},{6,4},{8,6},{10,8},{12,10},{14,12},{1,15},{3,1}... | collective-permute-start | bytes 393224 | tf_op jit(solution)/shard_map/ppermute | solution.py:176
  37.7 0.0 collective-permute-done.2.refs_2_
  37.8 2.1 %collective-permute-start.4 = (bf16[128,512]{1,0:T(8,128)(2,1)S(1)}, bf16[128,512]{1,0:T(8,128)(2,1)S(1)}, u32[]{:S(2)}, u32[]{:S(2)}) collective-permute-start(bf16[128,512]{1,0:T(8,128)(2,1)S(1)} %collective-permute-done.2.refs_2_), channel_id=1, source_target_pairs={{0,14},{2,0},{4,2},{6,4},{8,6},{10,8},{12,10},{14,12},{1,15},{3,1}... | collective-permute-start | bytes 393224 | tf_op jit(solution)/shard_map/ppermute | solution.py:176
  39.8 0.0 collective-permute-done.13.refs_15_
  39.8 0.0 collective-permute-start.14
  39.8 0.7 collective-permute-done.9.refs_12_
  40.5 2.9 %collective-permute-start.7 = (bf16[128,512]{1,0:T(8,128)(2,1)S(1)}, bf16[128,512]{1,0:T(8,128)(2,1)S(1)}, u32[]{:S(2)}, u32[]{:S(2)}) collective-permute-start(bf16[128,512]{1,0:T(8,128)(2,1)S(1)} %collective-permute-done.5.refs_5_), channel_id=1, source_target_pairs={{0,14},{2,0},{4,2},{6,4},{8,6},{10,8},{12,10},{14,12},{1,15},{3,1}... | collective-permute-start | bytes 393224 | tf_op jit(solution)/shard_map/ppermute | solution.py:176
  43.5 1.4 %collective-permute-start.6 = (bf16[128,512]{1,0:T(8,128)(2,1)S(1)}, bf16[128,512]{1,0:T(8,128)(2,1)S(1)}, u32[]{:S(2)}, u32[]{:S(2)}) collective-permute-start(bf16[128,512]{1,0:T(8,128)(2,1)S(1)} %collective-permute-done.4.refs_4_), channel_id=1, source_target_pairs={{0,14},{2,0},{4,2},{6,4},{8,6},{10,8},{12,10},{14,12},{1,15},{3,1}... | collective-permute-start | bytes 393224 | tf_op jit(solution)/shard_map/ppermute | solution.py:176
  44.9 0.3 collective-permute-done.14.refs_13_
  45.1 1.4 %collective-permute-done.10.refs_10_ = bf16[128,512]{1,0:T(8,128)(2,1)S(1)} collective-permute-done((bf16[128,512]{1,0:T(8,128)(2,1)S(1)}, bf16[128,512]{1,0:T(8,128)(2,1)S(1)}, u32[]{:S(2)}, u32[]{:S(2)}) %collective-permute-start.10) | collective-permute-done | bytes 131104 | tf_op jit(solution)/shard_map/ppermute | solution.py:176
  46.5 0.0 collective-permute-start.11
  46.5 0.0 collective-permute-done.7.refs_7_
  46.6 3.2 %collective-permute-start.12 = (bf16[128,512]{1,0:T(8,128)(2,1)S(1)}, bf16[128,512]{1,0:T(8,128)(2,1)S(1)}, u32[]{:S(2)}, u32[]{:S(2)}) collective-permute-start(bf16[128,512]{1,0:T(8,128)(2,1)S(1)} %collective-permute-done.7.refs_7_), channel_id=1, source_target_pairs={{0,14},{2,0},{4,2},{6,4},{8,6},{10,8},{12,10},{14,12},{1,15},{3,1}... | collective-permute-start | bytes 393224 | tf_op jit(solution)/shard_map/ppermute | solution.py:176
  49.8 2.0 %collective-permute-done.15.refs_11_ = bf16[128,512]{1,0:T(8,128)(2,1)S(1)} collective-permute-done((bf16[128,512]{1,0:T(8,128)(2,1)S(1)}, bf16[128,512]{1,0:T(8,128)(2,1)S(1)}, u32[]{:S(2)}, u32[]{:S(2)}) %collective-permute-start.15) | collective-permute-done | bytes 131104 | tf_op jit(solution)/shard_map/ppermute | solution.py:176
  51.9 1.6 %collective-permute-done.11.refs_8_ = bf16[128,512]{1,0:T(8,128)(2,1)S(1)} collective-permute-done((bf16[128,512]{1,0:T(8,128)(2,1)S(1)}, bf16[128,512]{1,0:T(8,128)(2,1)S(1)}, u32[]{:S(2)}, u32[]{:S(2)}) %collective-permute-start.11) | collective-permute-done | bytes 131104 | tf_op jit(solution)/shard_map/ppermute | solution.py:176
  53.4 2.7 %shard_map.66 = (f32[512,256]{1,0:T(8,128)S(1)}, f32[512,256]{1,0:T(8,128)S(1)}, f32[128,2,256]{2,1,0:T(2,128)S(1)}) custom-call(bf16[494,4096]{1,0:T(8,128)(2,1)S(1)} %bitcast.8, bf16[494,4096]{1,0:T(8,128)(2,1)S(1)} %bitcast.11, bf16[128,512]{1,0:T(8,128)(2,1)S(1)} %get-tuple-element.61.refs_0_, bf16[128,512]{1,0:T(8,128)(2,1)S(1)} %get-tuple-element.62.refs_1_, ...), custom_call_target="tpu_custom_call" | custom-call | tf_op jit(solution)/shard_map/pallas_call | solution.py:254
  56.1 22.2 %all_to_all.16.stats_ref = f32[128,2,256]{2,1,0:T(2,128)S(1)} all-to-all(f32[128,2,256]{2,1,0:T(2,128)S(1)} %get-tuple-element.63), channel_id=1, replica_groups=mesh['y'=4,'x'=4,'z'=8,'c'=2] {'y','x','z'}, dimensions={0} | all-to-all | bytes 524288 | tf_op jit(solution)/shard_map/all_to_all | solution.py:267
  78.3 1.4 %shard_map.67 = (bf16[256,512]{1,0:T(8,128)(2,1)S(1)}, bf16[256,512]{1,0:T(8,128)(2,1)S(1)}, f32[128,512]{1,0:T(8,128)S(1)}, f32[128,512]{1,0:T(8,128)S(1)}, f32...) custom-call(f32[128,2,256]{2,1,0:T(2,128)S(1)} %all_to_all.16.stats_ref, ...), custom_call_target="tpu_custom_call" | custom-call | tf_op jit(solution)/shard_map/pallas_call | solution.py:271
  79.7 0.0 copy-start.1
  79.7 1.5 %shard_map.68 = (f32[128,512]{1,0:T(8,128)S(1)}, f32[128,512]{1,0:T(8,128)S(1)}, f32[128,512]{1,0:T(8,128)S(1)}, f32[128,512]{1,0:T(8,128)S(1)}, f32[128,512]{1,...) custom-call(bf16[256,512]{1,0:T(8,128)(2,1)S(1)} %get-tuple-element., ...), custom_call_target="tpu_custom_call" | custom-call | tf_op jit(solution)/shard_map/pallas_call | solution.py:278
  81.3 0.7 copy-done
  82.0 0.3 collective-permute-start.19
  82.3 2.5 %collective-permute-start.16 = (f16[128,512]{1,0:T(8,128)(2,1)S(1)}, f16[128,512]{1,0:T(8,128)(2,1)S(1)}, u32[]{:S(2)}, u32[]{:S(2)}) collective-permute-start(f16[128,512]{1,0:T(8,128)(2,1)S(1)} %convert_element_type.92), channel_id=1, source_target_pairs={{0,14},{2,0},{4,2},{6,4},{8,6},{10,8},{12,10},{14,12},{1,15},{3,1}... | collective-permute-start | bytes 393224 | tf_op jit(solution)/shard_map/ppermute | solution.py:176
  84.8 0.1 collective-permute-start.26
  84.9 1.5 %collective-permute-start.23 = (f16[128,512]{1,0:T(8,128)(2,1)S(1)}, f16[128,512]{1,0:T(8,128)(2,1)S(1)}, u32[]{:S(2)}, u32[]{:S(2)}) collective-permute-start(f16[128,512]{1,0:T(8,128)(2,1)S(1)} %convert_element_type.106), channel_id=1, source_target_pairs={{0,2},{2,4},{4,6},{6,8},{8,10},{10,12},{12,14},{14,0},{1,3},{3,5},... | collective-permute-start | bytes 393224 | tf_op jit(solution)/shard_map/ppermute | solution.py:176
  86.4 0.7 collective-permute-done.19
  87.1 1.0 add_convert_fusion.7
  88.1 0.1 collective-permute-start.20
  88.2 1.0 add_convert_fusion.9
  89.2 2.7 %collective-permute-start.17 = (f16[128,512]{1,0:T(8,128)(2,1)S(1)}, f16[128,512]{1,0:T(8,128)(2,1)S(1)}, u32[]{:S(2)}, u32[]{:S(2)}) collective-permute-start(f16[128,512]{1,0:T(8,128)(2,1)S(1)} %add_convert_fusion.9), channel_id=1, source_target_pairs={{0,14},{2,0},{4,2},{6,4},{8,6},{10,8},{12,10},{14,12},{1,15},{3,1}... | collective-permute-start | bytes 393224 | tf_op jit(solution)/shard_map/ppermute | solution.py:176
  92.0 0.1 collective-permute-start.27
  92.2 1.7 %collective-permute-start.24 = (f16[128,512]{1,0:T(8,128)(2,1)S(1)}, f16[128,512]{1,0:T(8,128)(2,1)S(1)}, u32[]{:S(2)}, u32[]{:S(2)}) collective-permute-start(f16[128,512]{1,0:T(8,128)(2,1)S(1)} %add_convert_fusion.4), channel_id=1, source_target_pairs={{0,2},{2,4},{4,6},{6,8},{8,10},{10,12},{12,14},{14,0},{1,3},{3,5},... | collective-permute-start | bytes 393224 | tf_op jit(solution)/shard_map/ppermute | solution.py:176
  94.0 0.1 collective-permute-start.21
  94.1 3.4 %collective-permute-start.18 = (f16[128,512]{1,0:T(8,128)(2,1)S(1)}, f16[128,512]{1,0:T(8,128)(2,1)S(1)}, u32[]{:S(2)}, u32[]{:S(2)}) collective-permute-start(f16[128,512]{1,0:T(8,128)(2,1)S(1)} %add_convert_fusion.8), channel_id=1, source_target_pairs={{0,14},{2,0},{4,2},{6,4},{8,6},{10,8},{12,10},{14,12},{1,15},{3,1}... | collective-permute-start | bytes 393224 | tf_op jit(solution)/shard_map/ppermute | solution.py:176
  97.5 2.8 %collective-permute-start.28 = (f16[128,512]{1,0:T(8,128)(2,1)S(1)}, f16[128,512]{1,0:T(8,128)(2,1)S(1)}, u32[]{:S(2)}, u32[]{:S(2)}) collective-permute-start(f16[128,512]{1,0:T(8,128)(2,1)S(1)} %add_convert_fusion.1), channel_id=1, source_target_pairs={{0,14},{2,0},{4,2},{6,4},{8,6},{10,8},{12,10},{14,12},{1,15},{3,1}... | collective-permute-start | bytes 393224 | tf_op jit(solution)/shard_map/ppermute | solution.py:176
  100.3 0.1 collective-permute-start.25
  100.4 0.0 collective-permute-done.21
  100.5 0.2 collective-permute-start.22
  100.7 1.5 %collective-permute-done.28 = f16[128,512]{1,0:T(8,128)(2,1)S(1)} collective-permute-done((f16[128,512]{1,0:T(8,128)(2,1)S(1)}, f16[128,512]{1,0:T(8,128)(2,1)S(1)}, u32[]{:S(2)}, u32[]{:S(2)}) %collective-permute-start.28) | collective-permute-done | bytes 131104 | tf_op jit(solution)/shard_map/ppermute | solution.py:176
  102.3 3.2 %collective-permute-start.29 = (f16[128,512]{1,0:T(8,128)(2,1)S(1)}, f16[128,512]{1,0:T(8,128)(2,1)S(1)}, u32[]{:S(2)}, u32[]{:S(2)}) collective-permute-start(f16[128,512]{1,0:T(8,128)(2,1)S(1)} %add_convert_fusion), channel_id=1, source_target_pairs={{0,14},{2,0},{4,2},{6,4},{8,6},{10,8},{12,10},{14,12},{1,15},{3,1}... | collective-permute-start | bytes 393224 | tf_op jit(solution)/shard_map/ppermute | solution.py:176
  105.4 1.7 %collective-permute-done.22 = f16[128,512]{1,0:T(8,128)(2,1)S(1)} collective-permute-done((f16[128,512]{1,0:T(8,128)(2,1)S(1)}, f16[128,512]{1,0:T(8,128)(2,1)S(1)}, u32[]{:S(2)}, u32[]{:S(2)}) %collective-permute-start.22) | collective-permute-done | bytes 131104 | tf_op jit(solution)/shard_map/ppermute | solution.py:176
  107.2 0.6 collective-permute-done.29
  107.9 1.1 shard_map.69
  109.0 0.1 convert_element_type.120
  109.1 11.6 %all_to_all.17 = f16[16,32,512]{2,1,0:T(8,128)(2,1)S(1)} all-to-all(f16[16,32,512]{2,1,0:T(8,128)(2,1)S(1)} %bitcast.16), channel_id=1, replica_groups=mesh['y'=4,'x'=4,'z'=8,'c'=2] {'y','x'}, dimensions={0} | all-to-all | bytes 1048576 | tf_op jit(solution)/shard_map/all_to_all | solution.py:299
  120.7 0.1 convert_reduce_fusion
  120.8 11.8 %collective-permute-start.30 = (f32[32,256]{1,0:T(8,128)S(1)}, f32[32,256]{1,0:T(8,128)S(1)}, u32[]{:S(2)}, u32[]{:S(2)}) collective-permute-start(f32[32,256]{1,0:T(8,128)S(1)} %get-tuple-element.103), channel_id=1, source_target_pairs={{0,1},{1,0},{2,3},{3,2},{4,5},{5,4},{6,7},{7,6},{8,9},{9,8},{10,11... | collective-permute-start | bytes 98312 | tf_op jit(solution)/shard_map/ppermute | solution.py:172
  132.6 0.9 collective-permute-done.30.got_ref
  133.5 1.5 %shard_map.70 = f32[1024,256]{1,0:T(8,128)} custom-call(s32[8,64]{1,0:T(8,128)S(1)} %copy-done.3, f32[32,256]{1,0:T(8,128)S(1)} %get-tuple-element.104.kept_ref, f32[32,256]{1,0:T(8,128)S(1)} %collective-permute-done.30.got_ref), custom_call_target="tpu_custom_call" | custom-call | tf_op jit(solution)/shard_map/pallas_call | solution.py:303
  (43 shorter events, 0.6 us)
Async XLA Ops:
  2.6 6.4 %collective-permute-start = (bf16[32,256]{1,0:T(8,128)(2,1)}, bf16[32,256]{1,0:T(8,128)(2,1)S(1)}, u32[]{:S(2)}, u32[]{:S(2)}) collective-permute-start(bf16[32,256]{1,0:T(8,128)(2,1)} %get-tuple-element.56), channel_id=1, source_target_pairs={{0,1},{1,0},{2,3},{3,2},{4,5},{5,4},{6,7},{7,6},{8,9},{9,8},{10,11... | collective-permute-start | bytes 49160 | tf_op jit(solution)/shard_map/ppermute | solution.py:172
  6.5 2.5 %copy-start.4 = (bf16[32,256]{1,0:T(8,128)(2,1)S(1)}, bf16[32,256]{1,0:T(8,128)(2,1)}, u32[]{:S(2)}) copy-start(bf16[32,256]{1,0:T(8,128)(2,1)} %get-tuple-element.55) | copy-start | bytes 49156
  6.5 2.5 %copy-start.5 = (bf16[32,128]{1,0:T(8,128)(2,1)S(1)}, bf16[32,128]{1,0:T(8,128)(2,1)}, u32[]{:S(2)}) copy-start(bf16[32,128]{1,0:T(8,128)(2,1)} %get-tuple-element.57) | copy-start | bytes 24580
  6.5 19.5 %copy-start.2 = (s32[16]{0:T(128)S(1)}, s32[16]{0:T(128)}, u32[]{:S(2)}) copy-start(s32[16]{0:T(128)} %counts_ref.5) | copy-start | bytes 196
  9.0 44.4 %collective-permute-start.1 = (bf16[4096,494]{0,1:T(8,128)(2,1)S(1)}, bf16[4096,494]{0,1:T(8,128)(2,1)S(1)}, u32[]{:S(2)}, u32[]{:S(2)}) collective-permute-start(bf16[4096,494]{0,1:T(8,128)(2,1)S(1)} %broadcast_select_fusion), channel_id=1, source_target_pairs={{0,1},{1,0},{2,3},{3,2},{4,5},{5,4},{6,7},{7,6},{8,9},{9,8},{10,11... | collective-permute-start | bytes 12140552 | tf_op jit(solution)/shard_map/ppermute | solution.py:172
  27.0 8.0 %collective-permute-start.8 = (bf16[128,512]{1,0:T(8,128)(2,1)S(1)}, bf16[128,512]{1,0:T(8,128)(2,1)S(1)}, u32[]{:S(2)}, u32[]{:S(2)}) collective-permute-start(bf16[128,512]{1,0:T(8,128)(2,1)S(1)} %get-tuple-element.61.refs_0_), channel_id=1, source_target_pairs={{0,2},{2,4},{4,6},{6,8},{8,10},{10,12},{12,14},{14,0},{1,3},{3,5},... | collective-permute-start | bytes 393224 | tf_op jit(solution)/shard_map/ppermute | solution.py:176
  28.7 6.3 %collective-permute-start.3 = (bf16[128,512]{1,0:T(8,128)(2,1)S(1)}, bf16[128,512]{1,0:T(8,128)(2,1)S(1)}, u32[]{:S(2)}, u32[]{:S(2)}) collective-permute-start(bf16[128,512]{1,0:T(8,128)(2,1)S(1)} %get-tuple-element.62.refs_1_), channel_id=1, source_target_pairs={{0,14},{2,0},{4,2},{6,4},{8,6},{10,8},{12,10},{14,12},{1,15},{3,1}... | collective-permute-start | bytes 393224 | tf_op jit(solution)/shard_map/ppermute | solution.py:176
  32.7 5.0 %collective-permute-start.2 = (bf16[128,512]{1,0:T(8,128)(2,1)S(1)}, bf16[128,512]{1,0:T(8,128)(2,1)S(1)}, u32[]{:S(2)}, u32[]{:S(2)}) collective-permute-start(bf16[128,512]{1,0:T(8,128)(2,1)S(1)} %get-tuple-element.61.refs_0_), channel_id=1, source_target_pairs={{0,14},{2,0},{4,2},{6,4},{8,6},{10,8},{12,10},{14,12},{1,15},{3,1}... | collective-permute-start | bytes 393224 | tf_op jit(solution)/shard_map/ppermute | solution.py:176
  34.1 5.7 %collective-permute-start.13 = (bf16[128,512]{1,0:T(8,128)(2,1)S(1)}, bf16[128,512]{1,0:T(8,128)(2,1)S(1)}, u32[]{:S(2)}, u32[]{:S(2)}) collective-permute-start(bf16[128,512]{1,0:T(8,128)(2,1)S(1)} %get-tuple-element.62.refs_1_), channel_id=1, source_target_pairs={{0,2},{2,4},{4,6},{6,8},{8,10},{10,12},{12,14},{14,0},{1,3},{3,5},... | collective-permute-start | bytes 393224 | tf_op jit(solution)/shard_map/ppermute | solution.py:176
  35.0 5.5 %collective-permute-start.9 = (bf16[128,512]{1,0:T(8,128)(2,1)S(1)}, bf16[128,512]{1,0:T(8,128)(2,1)S(1)}, u32[]{:S(2)}, u32[]{:S(2)}) collective-permute-start(bf16[128,512]{1,0:T(8,128)(2,1)S(1)} %collective-permute-done.8.refs_14_), channel_id=1, source_target_pairs={{0,2},{2,4},{4,6},{6,8},{8,10},{10,12},{12,14},{14,0},{1,3},{3,5},... | collective-permute-start | bytes 393224 | tf_op jit(solution)/shard_map/ppermute | solution.py:176
  35.0 5.5 %collective-permute-start.5 = (bf16[128,512]{1,0:T(8,128)(2,1)S(1)}, bf16[128,512]{1,0:T(8,128)(2,1)S(1)}, u32[]{:S(2)}, u32[]{:S(2)}) collective-permute-start(bf16[128,512]{1,0:T(8,128)(2,1)S(1)} %collective-permute-done.3.refs_3_), channel_id=1, source_target_pairs={{0,14},{2,0},{4,2},{6,4},{8,6},{10,8},{12,10},{14,12},{1,15},{3,1}... | collective-permute-start | bytes 393224 | tf_op jit(solution)/shard_map/ppermute | solution.py:176
  37.8 5.7 %collective-permute-start.4 = (bf16[128,512]{1,0:T(8,128)(2,1)S(1)}, bf16[128,512]{1,0:T(8,128)(2,1)S(1)}, u32[]{:S(2)}, u32[]{:S(2)}) collective-permute-start(bf16[128,512]{1,0:T(8,128)(2,1)S(1)} %collective-permute-done.2.refs_2_), channel_id=1, source_target_pairs={{0,14},{2,0},{4,2},{6,4},{8,6},{10,8},{12,10},{14,12},{1,15},{3,1}... | collective-permute-start | bytes 393224 | tf_op jit(solution)/shard_map/ppermute | solution.py:176
  39.8 5.3 %collective-permute-start.14 = (bf16[128,512]{1,0:T(8,128)(2,1)S(1)}, bf16[128,512]{1,0:T(8,128)(2,1)S(1)}, u32[]{:S(2)}, u32[]{:S(2)}) collective-permute-start(bf16[128,512]{1,0:T(8,128)(2,1)S(1)} %collective-permute-done.13.refs_15_), channel_id=1, source_target_pairs={{0,2},{2,4},{4,6},{6,8},{8,10},{10,12},{12,14},{14,0},{1,3},{3,5},... | collective-permute-start | bytes 393224 | tf_op jit(solution)/shard_map/ppermute | solution.py:176
  40.5 6.0 %collective-permute-start.10 = (bf16[128,512]{1,0:T(8,128)(2,1)S(1)}, bf16[128,512]{1,0:T(8,128)(2,1)S(1)}, u32[]{:S(2)}, u32[]{:S(2)}) collective-permute-start(bf16[128,512]{1,0:T(8,128)(2,1)S(1)} %collective-permute-done.9.refs_12_), channel_id=1, source_target_pairs={{0,2},{2,4},{4,6},{6,8},{8,10},{10,12},{12,14},{14,0},{1,3},{3,5},... | collective-permute-start | bytes 393224 | tf_op jit(solution)/shard_map/ppermute | solution.py:176
  40.5 6.0 %collective-permute-start.7 = (bf16[128,512]{1,0:T(8,128)(2,1)S(1)}, bf16[128,512]{1,0:T(8,128)(2,1)S(1)}, u32[]{:S(2)}, u32[]{:S(2)}) collective-permute-start(bf16[128,512]{1,0:T(8,128)(2,1)S(1)} %collective-permute-done.5.refs_5_), channel_id=1, source_target_pairs={{0,14},{2,0},{4,2},{6,4},{8,6},{10,8},{12,10},{14,12},{1,15},{3,1}... | collective-permute-start | bytes 393224 | tf_op jit(solution)/shard_map/ppermute | solution.py:176
  43.5 6.3 %collective-permute-start.6 = (bf16[128,512]{1,0:T(8,128)(2,1)S(1)}, bf16[128,512]{1,0:T(8,128)(2,1)S(1)}, u32[]{:S(2)}, u32[]{:S(2)}) collective-permute-start(bf16[128,512]{1,0:T(8,128)(2,1)S(1)} %collective-permute-done.4.refs_4_), channel_id=1, source_target_pairs={{0,14},{2,0},{4,2},{6,4},{8,6},{10,8},{12,10},{14,12},{1,15},{3,1}... | collective-permute-start | bytes 393224 | tf_op jit(solution)/shard_map/ppermute | solution.py:176
  45.1 6.7 %collective-permute-start.15 = (bf16[128,512]{1,0:T(8,128)(2,1)S(1)}, bf16[128,512]{1,0:T(8,128)(2,1)S(1)}, u32[]{:S(2)}, u32[]{:S(2)}) collective-permute-start(bf16[128,512]{1,0:T(8,128)(2,1)S(1)} %collective-permute-done.14.refs_13_), channel_id=1, source_target_pairs={{0,2},{2,4},{4,6},{6,8},{8,10},{10,12},{12,14},{14,0},{1,3},{3,5},... | collective-permute-start | bytes 393224 | tf_op jit(solution)/shard_map/ppermute | solution.py:176
  46.5 6.9 %collective-permute-start.11 = (bf16[128,512]{1,0:T(8,128)(2,1)S(1)}, bf16[128,512]{1,0:T(8,128)(2,1)S(1)}, u32[]{:S(2)}, u32[]{:S(2)}) collective-permute-start(bf16[128,512]{1,0:T(8,128)(2,1)S(1)} %collective-permute-done.10.refs_10_), channel_id=1, source_target_pairs={{0,2},{2,4},{4,6},{6,8},{8,10},{10,12},{12,14},{14,0},{1,3},{3,5},... | collective-permute-start | bytes 393224 | tf_op jit(solution)/shard_map/ppermute | solution.py:176
  46.6 6.9 %collective-permute-start.12 = (bf16[128,512]{1,0:T(8,128)(2,1)S(1)}, bf16[128,512]{1,0:T(8,128)(2,1)S(1)}, u32[]{:S(2)}, u32[]{:S(2)}) collective-permute-start(bf16[128,512]{1,0:T(8,128)(2,1)S(1)} %collective-permute-done.7.refs_7_), channel_id=1, source_target_pairs={{0,14},{2,0},{4,2},{6,4},{8,6},{10,8},{12,10},{14,12},{1,15},{3,1}... | collective-permute-start | bytes 393224 | tf_op jit(solution)/shard_map/ppermute | solution.py:176
  79.7 1.5 %copy-start.1 = (f32[128,512]{1,0:T(8,128)}, f32[128,512]{1,0:T(8,128)S(1)}, u32[]{:S(2)}) copy-start(f32[128,512]{1,0:T(8,128)S(1)} %get-tuple-element.90) | copy-start | bytes 786436
  81.3 0.7 copy-start
  82.0 5.1 %collective-permute-start.19 = (f16[128,512]{1,0:T(8,128)(2,1)S(1)}, f16[128,512]{1,0:T(8,128)(2,1)}, u32[]{:S(2)}, u32[]{:S(2)}) collective-permute-start(f16[128,512]{1,0:T(8,128)(2,1)S(1)} %convert_element_type.98), channel_id=1, source_target_pairs={{0,2},{2,4},{4,6},{6,8},{8,10},{10,12},{12,14},{14,0},{1,3},{3,5},... | collective-permute-start | bytes 393224 | tf_op jit(solution)/shard_map/ppermute | solution.py:176
  82.3 5.9 %collective-permute-start.16 = (f16[128,512]{1,0:T(8,128)(2,1)S(1)}, f16[128,512]{1,0:T(8,128)(2,1)S(1)}, u32[]{:S(2)}, u32[]{:S(2)}) collective-permute-start(f16[128,512]{1,0:T(8,128)(2,1)S(1)} %convert_element_type.92), channel_id=1, source_target_pairs={{0,14},{2,0},{4,2},{6,4},{8,6},{10,8},{12,10},{14,12},{1,15},{3,1}... | collective-permute-start | bytes 393224 | tf_op jit(solution)/shard_map/ppermute | solution.py:176
  84.8 7.2 %collective-permute-start.26 = (f16[128,512]{1,0:T(8,128)(2,1)S(1)}, f16[128,512]{1,0:T(8,128)(2,1)S(1)}, u32[]{:S(2)}, u32[]{:S(2)}) collective-permute-start(f16[128,512]{1,0:T(8,128)(2,1)S(1)} %convert_element_type.112), channel_id=1, source_target_pairs={{0,14},{2,0},{4,2},{6,4},{8,6},{10,8},{12,10},{14,12},{1,15},{3,1}... | collective-permute-start | bytes 393224 | tf_op jit(solution)/shard_map/ppermute | solution.py:176
  84.9 7.2 %collective-permute-start.23 = (f16[128,512]{1,0:T(8,128)(2,1)S(1)}, f16[128,512]{1,0:T(8,128)(2,1)S(1)}, u32[]{:S(2)}, u32[]{:S(2)}) collective-permute-start(f16[128,512]{1,0:T(8,128)(2,1)S(1)} %convert_element_type.106), channel_id=1, source_target_pairs={{0,2},{2,4},{4,6},{6,8},{8,10},{10,12},{12,14},{14,0},{1,3},{3,5},... | collective-permute-start | bytes 393224 | tf_op jit(solution)/shard_map/ppermute | solution.py:176
  88.1 5.8 %collective-permute-start.20 = (f16[128,512]{1,0:T(8,128)(2,1)S(1)}, f16[128,512]{1,0:T(8,128)(2,1)S(1)}, u32[]{:S(2)}, u32[]{:S(2)}) collective-permute-start(f16[128,512]{1,0:T(8,128)(2,1)S(1)} %add_convert_fusion.7), channel_id=1, source_target_pairs={{0,2},{2,4},{4,6},{6,8},{8,10},{10,12},{12,14},{14,0},{1,3},{3,5},... | collective-permute-start | bytes 393224 | tf_op jit(solution)/shard_map/ppermute | solution.py:176
  89.2 4.8 %collective-permute-start.17 = (f16[128,512]{1,0:T(8,128)(2,1)S(1)}, f16[128,512]{1,0:T(8,128)(2,1)S(1)}, u32[]{:S(2)}, u32[]{:S(2)}) collective-permute-start(f16[128,512]{1,0:T(8,128)(2,1)S(1)} %add_convert_fusion.9), channel_id=1, source_target_pairs={{0,14},{2,0},{4,2},{6,4},{8,6},{10,8},{12,10},{14,12},{1,15},{3,1}... | collective-permute-start | bytes 393224 | tf_op jit(solution)/shard_map/ppermute | solution.py:176
  92.0 5.5 %collective-permute-start.27 = (f16[128,512]{1,0:T(8,128)(2,1)S(1)}, f16[128,512]{1,0:T(8,128)(2,1)S(1)}, u32[]{:S(2)}, u32[]{:S(2)}) collective-permute-start(f16[128,512]{1,0:T(8,128)(2,1)S(1)} %add_convert_fusion.2), channel_id=1, source_target_pairs={{0,14},{2,0},{4,2},{6,4},{8,6},{10,8},{12,10},{14,12},{1,15},{3,1}... | collective-permute-start | bytes 393224 | tf_op jit(solution)/shard_map/ppermute | solution.py:176
  92.2 8.1 %collective-permute-start.24 = (f16[128,512]{1,0:T(8,128)(2,1)S(1)}, f16[128,512]{1,0:T(8,128)(2,1)S(1)}, u32[]{:S(2)}, u32[]{:S(2)}) collective-permute-start(f16[128,512]{1,0:T(8,128)(2,1)S(1)} %add_convert_fusion.4), channel_id=1, source_target_pairs={{0,2},{2,4},{4,6},{6,8},{8,10},{10,12},{12,14},{14,0},{1,3},{3,5},... | collective-permute-start | bytes 393224 | tf_op jit(solution)/shard_map/ppermute | solution.py:176
  94.0 6.5 %collective-permute-start.21 = (f16[128,512]{1,0:T(8,128)(2,1)S(1)}, f16[128,512]{1,0:T(8,128)(2,1)S(1)}, u32[]{:S(2)}, u32[]{:S(2)}) collective-permute-start(f16[128,512]{1,0:T(8,128)(2,1)S(1)} %add_convert_fusion.6), channel_id=1, source_target_pairs={{0,2},{2,4},{4,6},{6,8},{8,10},{10,12},{12,14},{14,0},{1,3},{3,5},... | collective-permute-start | bytes 393224 | tf_op jit(solution)/shard_map/ppermute | solution.py:176
  94.1 11.3 %collective-permute-start.18 = (f16[128,512]{1,0:T(8,128)(2,1)S(1)}, f16[128,512]{1,0:T(8,128)(2,1)S(1)}, u32[]{:S(2)}, u32[]{:S(2)}) collective-permute-start(f16[128,512]{1,0:T(8,128)(2,1)S(1)} %add_convert_fusion.8), channel_id=1, source_target_pairs={{0,14},{2,0},{4,2},{6,4},{8,6},{10,8},{12,10},{14,12},{1,15},{3,1}... | collective-permute-start | bytes 393224 | tf_op jit(solution)/shard_map/ppermute | solution.py:176
  97.5 36.0 %copy-start.3 = (s32[8,64]{1,0:T(8,128)S(1)}, s32[8,64]{1,0:T(8,128)}, u32[]{:S(2)}) copy-start(s32[8,64]{1,0:T(8,128)} %get-tuple-element.54.places_ref) | copy-start | bytes 6148
  97.5 4.7 %collective-permute-start.28 = (f16[128,512]{1,0:T(8,128)(2,1)S(1)}, f16[128,512]{1,0:T(8,128)(2,1)S(1)}, u32[]{:S(2)}, u32[]{:S(2)}) collective-permute-start(f16[128,512]{1,0:T(8,128)(2,1)S(1)} %add_convert_fusion.1), channel_id=1, source_target_pairs={{0,14},{2,0},{4,2},{6,4},{8,6},{10,8},{12,10},{14,12},{1,15},{3,1}... | collective-permute-start | bytes 393224 | tf_op jit(solution)/shard_map/ppermute | solution.py:176
  100.3 6.9 %collective-permute-start.25 = (f16[128,512]{1,0:T(8,128)(2,1)S(1)}, f16[128,512]{1,0:T(8,128)(2,1)S(1)}, u32[]{:S(2)}, u32[]{:S(2)}) collective-permute-start(f16[128,512]{1,0:T(8,128)(2,1)S(1)} %add_convert_fusion.3), channel_id=1, source_target_pairs={{0,2},{2,4},{4,6},{6,8},{8,10},{10,12},{12,14},{14,0},{1,3},{3,5},... | collective-permute-start | bytes 393224 | tf_op jit(solution)/shard_map/ppermute | solution.py:176
  100.5 6.7 %collective-permute-start.22 = (f16[128,512]{1,0:T(8,128)(2,1)S(1)}, f16[128,512]{1,0:T(8,128)(2,1)S(1)}, u32[]{:S(2)}, u32[]{:S(2)}) collective-permute-start(f16[128,512]{1,0:T(8,128)(2,1)S(1)} %add_convert_fusion.5), channel_id=1, source_target_pairs={{0,2},{2,4},{4,6},{6,8},{8,10},{10,12},{12,14},{14,0},{1,3},{3,5},... | collective-permute-start | bytes 393224 | tf_op jit(solution)/shard_map/ppermute | solution.py:176
  102.3 5.6 %collective-permute-start.29 = (f16[128,512]{1,0:T(8,128)(2,1)S(1)}, f16[128,512]{1,0:T(8,128)(2,1)S(1)}, u32[]{:S(2)}, u32[]{:S(2)}) collective-permute-start(f16[128,512]{1,0:T(8,128)(2,1)S(1)} %add_convert_fusion), channel_id=1, source_target_pairs={{0,14},{2,0},{4,2},{6,4},{8,6},{10,8},{12,10},{14,12},{1,15},{3,1}... | collective-permute-start | bytes 393224 | tf_op jit(solution)/shard_map/ppermute | solution.py:176
  120.8 12.7 %collective-permute-start.30 = (f32[32,256]{1,0:T(8,128)S(1)}, f32[32,256]{1,0:T(8,128)S(1)}, u32[]{:S(2)}, u32[]{:S(2)}) collective-permute-start(f32[32,256]{1,0:T(8,128)S(1)} %get-tuple-element.103), channel_id=1, source_target_pairs={{0,1},{1,0},{2,3},{3,2},{4,5},{5,4},{6,7},{7,6},{8,9},{9,8},{10,11... | collective-permute-start | bytes 98312 | tf_op jit(solution)/shard_map/ppermute | solution.py:172
where the time goes:
time: 135 us
  starting transfers between devices  53.5 us (40%)
  blocking collectives  50.6 us (37%)
  waiting for transfers between devices  12.3 us (9%)
  Pallas kernels  11.2 us (8%)
  other arithmetic  5.13 us (4%)
  between operations  1.6 us (1%)
    ppermute x28, starting transfers between devices, pass_on(): return lax.ppermute(x, 'z', [(i, (i + by) % DEEP) for i in range(DEEP)])  38.3 us
    all_to_all x1, blocking collectives, local(): stats = lax.all_to_all(stats, CHIPS, 0, 0, tiled=True)  22.2 us
    all_to_all x1, blocking collectives, local(): lax.all_to_all(jnp.broadcast_to(slots[None], (SEQS,) + slots.shape), PLAN...  16.8 us
    ppermute x3, starting transfers between devices, swap_cores(): return lax.ppermute(x, 'c', [(0, 1), (1, 0)])  15.2 us
    all_to_all x1, blocking collectives, local(): back = lax.all_to_all(back, PLANE, 0, 0, tiled=True)  11.6 us
    ppermute x28, waiting for transfers between devices, pass_on(): return lax.ppermute(x, 'z', [(i, (i + by) % DEEP) for i in range(DEEP)])  11.5 us
  transfers between devices with their start and end apart: 31, of which 11 were waited for; matrix products, arithmetic and copies ran while one was open for 4% of the time, Pallas kernels for 1%

commit v1 on v0

--- a/solution.py
+++ b/solution.py
@@ -295,7 +295,7 @@
         compiler_params=small,
     )(counts, low, high)
     back = back.astype(jnp.float16).reshape(SEQS, SLOTS, span)
-    back, first_core = lax.optimization_barrier((back, c == 0))
+    first_core = c == 0
     back = lax.all_to_all(back, PLANE, 0, 0, tiled=True)
     back = jnp.sum(back.astype(jnp.float32), axis=0) * (1.0 / SENT_SCALE)
     kept = jnp.where(first_core, back[:, :feat], back[:, feat:])

time: 135 us -> 136 us (level)
  blocking collectives: 50.6 us -> 39 us
  waiting for transfers between devices: 12.3 us -> 23.4 us
  starting transfers between devices: 53.5 us -> 56.9 us
    all_to_all x1 -> x0, blocking collectives: 11.6 us -> none  [local(): back = lax.all_to_all(back, PLANE, 0, 0, tiled=True)]
    all_to_all x0 -> x1, waiting for transfers between devices: none -> 8.95 us  [local(): back = lax.all_to_all(back, PLANE, 0, 0, tiled=True)]
    all_to_all x0 -> x1, starting transfers between devices: none -> 3.57 us  [local(): back = lax.all_to_all(back, PLANE, 0, 0, tiled=True)]
    ppermute x28, starting transfers between devices: 38.3 us -> 36.1 us  [pass_on(): return lax.ppermute(x, 'z', [(i, (i + by) % DEEP) for i in range(DEEP)])]
    ppermute x28, waiting for transfers between devices: 11.5 us -> 13.6 us  [pass_on(): return lax.ppermute(x, 'z', [(i, (i + by) % DEEP) for i in range(DEEP)])]
    ppermute x3, starting transfers between devices: 15.2 us -> 17.2 us  [swap_cores(): return lax.ppermute(x, 'c', [(0, 1), (1, 0)])]
    convert_element_type x14, other arithmetic: 2.4 us -> 0.46 us  [send(): return pass_on(x.astype(jnp.float16), by).astype(jnp.float32)]
  transfers between devices with their start and end apart: 31 -> 32, of which waited for: 11 -> 15; matrix products, arithmetic and copies ran while one was open for 4% -> 2% of each run, Pallas kernels for 1% -> 1%
where the time goes in v1:
time: 136 us
  starting transfers between devices  56.9 us (42%)
  blocking collectives  39 us (29%)
  waiting for transfers between devices  23.4 us (17%)
  Pallas kernels  11.2 us (8%)
  other arithmetic  3.99 us (3%)
  between operations  1.6 us (1%)
    ppermute x28, starting transfers between devices, pass_on(): return lax.ppermute(x, 'z', [(i, (i + by) % DEEP) for i in range(DEEP)])  36.1 us
    all_to_all x1, blocking collectives, local(): stats = lax.all_to_all(stats, CHIPS, 0, 0, tiled=True)  22.2 us
    ppermute x3, starting transfers between devices, swap_cores(): return lax.ppermute(x, 'c', [(0, 1), (1, 0)])  17.2 us
    all_to_all x1, blocking collectives, local(): lax.all_to_all(jnp.broadcast_to(slots[None], (SEQS,) + slots.shape), PLAN...  16.8 us
    ppermute x28, waiting for transfers between devices, pass_on(): return lax.ppermute(x, 'z', [(i, (i + by) % DEEP) for i in range(DEEP)])  13.6 us
    all_to_all x1, waiting for transfers between devices, local(): back = lax.all_to_all(back, PLANE, 0, 0, tiled=True)  8.95 us
    all_to_all x1, starting transfers between devices, local(): back = lax.all_to_all(back, PLANE, 0, 0, tiled=True)  3.57 us
  transfers between devices with their start and end apart: 32, of which 15 were waited for; matrix products, arithmetic and copies ran while one was open for 2% of the time, Pallas kernels for 1%

profile of v1, /device:TPU:1, one launch (start us, length us, event | category | flops | bytes accessed | tf_op | source)
XLA Modules:
  0.0 136.1 jit_solution(7995647470593369339)
XLA Ops:
  0.7 2.0 %shard_map.64 = (bf16[32,256]{1,0:T(8,128)(2,1)}, bf16[32,128]{1,0:T(8,128)(2,1)}, bf16[32,256]{1,0:T(8,128)(2,1)}, s32[8,64]{1,0:T(8,128)}) custom-call(s32[16]{0:T(128)} %counts_ref.5, s32[1]{0:T(128)S(6)} %copy.7.ratio_ref, s32[1,1024]{1,0:T(1,128)} %positions_ref.1, s32[1,1024]{1,0:T(1,128)} %targets_ref.1, bf16[1024,256]{1,0:T(8,128)(2,1)} %bitcast.16), custom_call_target="tpu_custom_call" | custom-call | tf_op jit(solution)/shard_map/pallas_call | solution.py:221
  2.6 3.2 %collective-permute-start = (bf16[32,256]{1,0:T(8,128)(2,1)}, bf16[32,256]{1,0:T(8,128)(2,1)S(1)}, u32[]{:S(2)}, u32[]{:S(2)}) collective-permute-start(bf16[32,256]{1,0:T(8,128)(2,1)} %get-tuple-element.54), channel_id=1, source_target_pairs={{0,1},{1,0},{2,3},{3,2},{4,5},{5,4},{6,7},{7,6},{8,9},{9,8},{10,11... | collective-permute-start | bytes 49160 | tf_op jit(solution)/shard_map/ppermute | solution.py:172
  6.5 0.0 copy-start.2
  6.6 2.4 %broadcast_select_fusion = bf16[4096,494]{0,1:T(8,128)(2,1)S(1)} fusion(bf16[4096,494]{0,1:T(8,128)(2,1)} %param.11, pred[]{:T(512)} %bitcast.1), kind=kLoop, calls=%fused_computation | loop fusion | flops 2023424 | bytes 8093697 | tf_op jit(solution)/shard_map/jit(_where)/select_n | solution.py:237
  9.0 0.0 collective-permute-done
  9.0 0.1 collective-permute-start.1
  9.1 0.1 broadcast_in_dim.14
  9.2 16.8 %all_to_all.15 = bf16[16,32,640]{2,1,0:T(8,128)(2,1)S(1)} all-to-all(bf16[16,32,640]{2,1,0:T(8,128)(2,1)S(1)} %broadcast_in_dim.14), channel_id=1, replica_groups=mesh['y'=4,'x'=4,'z'=8,'c'=2] {'y','x'}, dimensions={0} | all-to-all | bytes 1310720 | tf_op jit(solution)/shard_map/all_to_all | solution.py:240
  26.0 1.0 shard_map.65
  27.0 1.7 %collective-permute-start.8 = (bf16[128,512]{1,0:T(8,128)(2,1)S(1)}, bf16[128,512]{1,0:T(8,128)(2,1)S(1)}, u32[]{:S(2)}, u32[]{:S(2)}) collective-permute-start(bf16[128,512]{1,0:T(8,128)(2,1)S(1)} %get-tuple-element.59.refs_0_), channel_id=1, source_target_pairs={{0,2},{2,4},{4,6},{6,8},{8,10},{10,12},{12,14},{14,0},{1,3},{3,5},... | collective-permute-start | bytes 393224 | tf_op jit(solution)/shard_map/ppermute | solution.py:176
  28.7 4.0 %collective-permute-start.3 = (bf16[128,512]{1,0:T(8,128)(2,1)S(1)}, bf16[128,512]{1,0:T(8,128)(2,1)S(1)}, u32[]{:S(2)}, u32[]{:S(2)}) collective-permute-start(bf16[128,512]{1,0:T(8,128)(2,1)S(1)} %get-tuple-element.60.refs_1_), channel_id=1, source_target_pairs={{0,14},{2,0},{4,2},{6,4},{8,6},{10,8},{12,10},{14,12},{1,15},{3,1}... | collective-permute-start | bytes 393224 | tf_op jit(solution)/shard_map/ppermute | solution.py:176
  32.7 1.4 %collective-permute-start.2 = (bf16[128,512]{1,0:T(8,128)(2,1)S(1)}, bf16[128,512]{1,0:T(8,128)(2,1)S(1)}, u32[]{:S(2)}, u32[]{:S(2)}) collective-permute-start(bf16[128,512]{1,0:T(8,128)(2,1)S(1)} %get-tuple-element.59.refs_0_), channel_id=1, source_target_pairs={{0,14},{2,0},{4,2},{6,4},{8,6},{10,8},{12,10},{14,12},{1,15},{3,1}... | collective-permute-start | bytes 393224 | tf_op jit(solution)/shard_map/ppermute | solution.py:176
  34.1 0.1 collective-permute-start.13
  34.2 0.8 collective-permute-done.8.refs_14_
  35.0 0.0 collective-permute-start.9
  35.0 0.0 collective-permute-done.3.refs_3_
  35.0 2.8 %collective-permute-start.5 = (bf16[128,512]{1,0:T(8,128)(2,1)S(1)}, bf16[128,512]{1,0:T(8,128)(2,1)S(1)}, u32[]{:S(2)}, u32[]{:S(2)}) collective-permute-start(bf16[128,512]{1,0:T(8,128)(2,1)S(1)} %collective-permute-done.3.refs_3_), channel_id=1, source_target_pairs={{0,14},{2,0},{4,2},{6,4},{8,6},{10,8},{12,10},{14,12},{1,15},{3,1}... | collective-permute-start | bytes 393224 | tf_op jit(solution)/shard_map/ppermute | solution.py:176
  37.7 0.0 collective-permute-done.2.refs_2_
  37.8 2.1 %collective-permute-start.4 = (bf16[128,512]{1,0:T(8,128)(2,1)S(1)}, bf16[128,512]{1,0:T(8,128)(2,1)S(1)}, u32[]{:S(2)}, u32[]{:S(2)}) collective-permute-start(bf16[128,512]{1,0:T(8,128)(2,1)S(1)} %collective-permute-done.2.refs_2_), channel_id=1, source_target_pairs={{0,14},{2,0},{4,2},{6,4},{8,6},{10,8},{12,10},{14,12},{1,15},{3,1}... | collective-permute-start | bytes 393224 | tf_op jit(solution)/shard_map/ppermute | solution.py:176
  39.8 0.0 collective-permute-done.13.refs_15_
  39.8 0.0 collective-permute-start.14
  39.8 0.7 collective-permute-done.9.refs_12_
  40.5 2.9 %collective-permute-start.7 = (bf16[128,512]{1,0:T(8,128)(2,1)S(1)}, bf16[128,512]{1,0:T(8,128)(2,1)S(1)}, u32[]{:S(2)}, u32[]{:S(2)}) collective-permute-start(bf16[128,512]{1,0:T(8,128)(2,1)S(1)} %collective-permute-done.5.refs_5_), channel_id=1, source_target_pairs={{0,14},{2,0},{4,2},{6,4},{8,6},{10,8},{12,10},{14,12},{1,15},{3,1}... | collective-permute-start | bytes 393224 | tf_op jit(solution)/shard_map/ppermute | solution.py:176
  43.5 0.0 collective-permute-done.4.refs_4_
  43.5 1.4 %collective-permute-start.6 = (bf16[128,512]{1,0:T(8,128)(2,1)S(1)}, bf16[128,512]{1,0:T(8,128)(2,1)S(1)}, u32[]{:S(2)}, u32[]{:S(2)}) collective-permute-start(bf16[128,512]{1,0:T(8,128)(2,1)S(1)} %collective-permute-done.4.refs_4_), channel_id=1, source_target_pairs={{0,14},{2,0},{4,2},{6,4},{8,6},{10,8},{12,10},{14,12},{1,15},{3,1}... | collective-permute-start | bytes 393224 | tf_op jit(solution)/shard_map/ppermute | solution.py:176
  44.9 0.3 collective-permute-done.14.refs_13_
  45.1 0.0 collective-permute-start.15
  45.1 1.4 %collective-permute-done.10.refs_10_ = bf16[128,512]{1,0:T(8,128)(2,1)S(1)} collective-permute-done((bf16[128,512]{1,0:T(8,128)(2,1)S(1)}, bf16[128,512]{1,0:T(8,128)(2,1)S(1)}, u32[]{:S(2)}, u32[]{:S(2)}) %collective-permute-start.10) | collective-permute-done | bytes 131104 | tf_op jit(solution)/shard_map/ppermute | solution.py:176
  46.6 3.2 %collective-permute-start.12 = (bf16[128,512]{1,0:T(8,128)(2,1)S(1)}, bf16[128,512]{1,0:T(8,128)(2,1)S(1)}, u32[]{:S(2)}, u32[]{:S(2)}) collective-permute-start(bf16[128,512]{1,0:T(8,128)(2,1)S(1)} %collective-permute-done.7.refs_7_), channel_id=1, source_target_pairs={{0,14},{2,0},{4,2},{6,4},{8,6},{10,8},{12,10},{14,12},{1,15},{3,1}... | collective-permute-start | bytes 393224 | tf_op jit(solution)/shard_map/ppermute | solution.py:176
  49.8 2.1 %collective-permute-done.15.refs_11_ = bf16[128,512]{1,0:T(8,128)(2,1)S(1)} collective-permute-done((bf16[128,512]{1,0:T(8,128)(2,1)S(1)}, bf16[128,512]{1,0:T(8,128)(2,1)S(1)}, u32[]{:S(2)}, u32[]{:S(2)}) %collective-permute-start.15) | collective-permute-done | bytes 131104 | tf_op jit(solution)/shard_map/ppermute | solution.py:176
  51.9 1.6 %collective-permute-done.11.refs_8_ = bf16[128,512]{1,0:T(8,128)(2,1)S(1)} collective-permute-done((bf16[128,512]{1,0:T(8,128)(2,1)S(1)}, bf16[128,512]{1,0:T(8,128)(2,1)S(1)}, u32[]{:S(2)}, u32[]{:S(2)}) %collective-permute-start.11) | collective-permute-done | bytes 131104 | tf_op jit(solution)/shard_map/ppermute | solution.py:176
  53.5 2.7 %shard_map.66 = (f32[512,256]{1,0:T(8,128)S(1)}, f32[512,256]{1,0:T(8,128)S(1)}, f32[128,2,256]{2,1,0:T(2,128)S(1)}) custom-call(bf16[494,4096]{1,0:T(8,128)(2,1)S(1)} %bitcast.8, bf16[494,4096]{1,0:T(8,128)(2,1)S(1)} %bitcast.11, bf16[128,512]{1,0:T(8,128)(2,1)S(1)} %get-tuple-element.59.refs_0_, bf16[128,512]{1,0:T(8,128)(2,1)S(1)} %get-tuple-element.60.refs_1_, ...), custom_call_target="tpu_custom_call" | custom-call | tf_op jit(solution)/shard_map/pallas_call | solution.py:254
  56.2 22.2 %all_to_all.16.stats_ref = f32[128,2,256]{2,1,0:T(2,128)S(1)} all-to-all(f32[128,2,256]{2,1,0:T(2,128)S(1)} %get-tuple-element.61), channel_id=1, replica_groups=mesh['y'=4,'x'=4,'z'=8,'c'=2] {'y','x','z'}, dimensions={0} | all-to-all | bytes 524288 | tf_op jit(solution)/shard_map/all_to_all | solution.py:267
  78.3 1.4 %shard_map.67 = (bf16[256,512]{1,0:T(8,128)(2,1)S(1)}, bf16[256,512]{1,0:T(8,128)(2,1)S(1)}, f32[128,512]{1,0:T(8,128)S(1)}, f32[128,512]{1,0:T(8,128)S(1)}, f32...) custom-call(f32[128,2,256]{2,1,0:T(2,128)S(1)} %all_to_all.16.stats_ref, ...), custom_call_target="tpu_custom_call" | custom-call | tf_op jit(solution)/shard_map/pallas_call | solution.py:271
  79.7 1.6 %shard_map.68 = (f32[128,512]{1,0:T(8,128)S(1)}, f32[128,512]{1,0:T(8,128)S(1)}, f32[128,512]{1,0:T(8,128)S(1)}, f32[128,512]{1,0:T(8,128)S(1)}, f32[128,512]{1,...) custom-call(bf16[256,512]{1,0:T(8,128)(2,1)S(1)} %get-tuple-element., ...), custom_call_target="tpu_custom_call" | custom-call | tf_op jit(solution)/shard_map/pallas_call | solution.py:278
  81.3 0.4 collective-permute-start.19
  81.7 2.5 %collective-permute-start.16 = (f16[128,512]{1,0:T(8,128)(2,1)S(1)}, f16[128,512]{1,0:T(8,128)(2,1)S(1)}, u32[]{:S(2)}, u32[]{:S(2)}) collective-permute-start(f16[128,512]{1,0:T(8,128)(2,1)S(1)} %convert_element_type.92), channel_id=1, source_target_pairs={{0,14},{2,0},{4,2},{6,4},{8,6},{10,8},{12,10},{14,12},{1,15},{3,1}... | collective-permute-start | bytes 393224 | tf_op jit(solution)/shard_map/ppermute | solution.py:176
  84.2 0.1 collective-permute-start.26
  84.3 1.5 %collective-permute-start.23 = (f16[128,512]{1,0:T(8,128)(2,1)S(1)}, f16[128,512]{1,0:T(8,128)(2,1)S(1)}, u32[]{:S(2)}, u32[]{:S(2)}) collective-permute-start(f16[128,512]{1,0:T(8,128)(2,1)S(1)} %convert_element_type.106), channel_id=1, source_target_pairs={{0,2},{2,4},{4,6},{6,8},{8,10},{10,12},{12,14},{14,0},{1,3},{3,5},... | collective-permute-start | bytes 393224 | tf_op jit(solution)/shard_map/ppermute | solution.py:176
  85.9 0.6 collective-permute-done.19
  86.5 0.1 collective-permute-start.20
  86.6 2.7 %collective-permute-start.17 = (f16[128,512]{1,0:T(8,128)(2,1)S(1)}, f16[128,512]{1,0:T(8,128)(2,1)S(1)}, u32[]{:S(2)}, u32[]{:S(2)}) collective-permute-start(f16[128,512]{1,0:T(8,128)(2,1)S(1)} %add_convert_fusion.9), channel_id=1, source_target_pairs={{0,14},{2,0},{4,2},{6,4},{8,6},{10,8},{12,10},{14,12},{1,15},{3,1}... | collective-permute-start | bytes 393224 | tf_op jit(solution)/shard_map/ppermute | solution.py:176
  89.4 1.3 collective-permute-start.27
  90.8 0.5 collective-permute-start.24
  91.3 0.3 collective-permute-done.20
  91.6 0.1 collective-permute-start.21
  91.8 2.7 %collective-permute-start.18 = (f16[128,512]{1,0:T(8,128)(2,1)S(1)}, f16[128,512]{1,0:T(8,128)(2,1)S(1)}, u32[]{:S(2)}, u32[]{:S(2)}) collective-permute-start(f16[128,512]{1,0:T(8,128)(2,1)S(1)} %add_convert_fusion.8), channel_id=1, source_target_pairs={{0,14},{2,0},{4,2},{6,4},{8,6},{10,8},{12,10},{14,12},{1,15},{3,1}... | collective-permute-start | bytes 393224 | tf_op jit(solution)/shard_map/ppermute | solution.py:176
  94.6 1.3 collective-permute-start.28
  95.9 0.4 collective-permute-done.24
  96.4 0.1 collective-permute-start.25
  96.5 2.2 %collective-permute-done.21 = f16[128,512]{1,0:T(8,128)(2,1)S(1)} collective-permute-done((f16[128,512]{1,0:T(8,128)(2,1)S(1)}, f16[128,512]{1,0:T(8,128)(2,1)S(1)}, u32[]{:S(2)}, u32[]{:S(2)}) %collective-permute-start.21) | collective-permute-done | bytes 131104 | tf_op jit(solution)/shard_map/ppermute | solution.py:176
  98.7 0.1 collective-permute-start.22
  98.8 0.4 collective-permute-done.28
  99.2 3.1 %collective-permute-start.29 = (f16[128,512]{1,0:T(8,128)(2,1)S(1)}, f16[128,512]{1,0:T(8,128)(2,1)S(1)}, u32[]{:S(2)}, u32[]{:S(2)}) collective-permute-start(f16[128,512]{1,0:T(8,128)(2,1)S(1)} %add_convert_fusion), channel_id=1, source_target_pairs={{0,14},{2,0},{4,2},{6,4},{8,6},{10,8},{12,10},{14,12},{1,15},{3,1}... | collective-permute-start | bytes 393224 | tf_op jit(solution)/shard_map/ppermute | solution.py:176
  102.3 1.9 %collective-permute-done.22 = f16[128,512]{1,0:T(8,128)(2,1)S(1)} collective-permute-done((f16[128,512]{1,0:T(8,128)(2,1)S(1)}, f16[128,512]{1,0:T(8,128)(2,1)S(1)}, u32[]{:S(2)}, u32[]{:S(2)}) %collective-permute-start.22) | collective-permute-done | bytes 131104 | tf_op jit(solution)/shard_map/ppermute | solution.py:176
  104.3 0.8 collective-permute-done.29
  105.2 1.1 shard_map.69
  106.3 0.9 convert_element_type.120
  107.2 3.6 %all-to-all-start.2 = ((f16[16,32,512]{2,1,0:T(8,128)(2,1)}), f16[16,32,512]{2,1,0:T(8,128)(2,1)S(1)}, u32[]{:S(2)}, u32[]{:S(2)}) async-start(f16[16,32,512]{2,1,0:T(8,128)(2,1)} %bitcast.5), calls=%async_computation.2 | async-start | bytes 1048576 | tf_op jit(solution)/shard_map/all_to_all | solution.py:299
  110.8 8.9 %all-to-all-done.2 = f16[16,32,512]{2,1,0:T(8,128)(2,1)S(1)} async-done(((f16[16,32,512]{2,1,0:T(8,128)(2,1)}), f16[16,32,512]{2,1,0:T(8,128)(2,1)S(1)}, u32[]{:S(2)}, u32[]{:S(2)}) %all-to-all-start.2) | async-done | bytes 524320 | tf_op jit(solution)/shard_map/all_to_all | solution.py:299
  119.7 0.1 convert_reduce_fusion
  119.9 13.9 %collective-permute-start.30 = (f32[32,256]{1,0:T(8,128)S(1)}, f32[32,256]{1,0:T(8,128)S(1)}, u32[]{:S(2)}, u32[]{:S(2)}) collective-permute-start(f32[32,256]{1,0:T(8,128)S(1)} %get-tuple-element.99), channel_id=1, source_target_pairs={{0,1},{1,0},{2,3},{3,2},{4,5},{5,4},{6,7},{7,6},{8,9},{9,8},{10,11... | collective-permute-start | bytes 98312 | tf_op jit(solution)/shard_map/ppermute | solution.py:172
  133.7 0.9 collective-permute-done.30.got_ref
  134.6 1.5 %shard_map.70 = f32[1024,256]{1,0:T(8,128)} custom-call(s32[8,64]{1,0:T(8,128)S(1)} %copy-done.1, f32[32,256]{1,0:T(8,128)S(1)} %get-tuple-element.100.kept_ref, f32[32,256]{1,0:T(8,128)S(1)} %collective-permute-done.30.got_ref), custom_call_target="tpu_custom_call" | custom-call | tf_op jit(solution)/shard_map/pallas_call | solution.py:303
  (40 shorter events, 0.6 us)
Async XLA Ops:
  2.6 6.4 %collective-permute-start = (bf16[32,256]{1,0:T(8,128)(2,1)}, bf16[32,256]{1,0:T(8,128)(2,1)S(1)}, u32[]{:S(2)}, u32[]{:S(2)}) collective-permute-start(bf16[32,256]{1,0:T(8,128)(2,1)} %get-tuple-element.54), channel_id=1, source_target_pairs={{0,1},{1,0},{2,3},{3,2},{4,5},{5,4},{6,7},{7,6},{8,9},{9,8},{10,11... | collective-permute-start | bytes 49160 | tf_op jit(solution)/shard_map/ppermute | solution.py:172
  6.5 2.5 %copy-start.2 = (bf16[32,256]{1,0:T(8,128)(2,1)S(1)}, bf16[32,256]{1,0:T(8,128)(2,1)}, u32[]{:S(2)}) copy-start(bf16[32,256]{1,0:T(8,128)(2,1)} %get-tuple-element.53) | copy-start | bytes 49156
  6.5 2.5 %copy-start.3 = (bf16[32,128]{1,0:T(8,128)(2,1)S(1)}, bf16[32,128]{1,0:T(8,128)(2,1)}, u32[]{:S(2)}) copy-start(bf16[32,128]{1,0:T(8,128)(2,1)} %get-tuple-element.55) | copy-start | bytes 24580
  6.5 19.5 %copy-start = (s32[16]{0:T(128)S(1)}, s32[16]{0:T(128)}, u32[]{:S(2)}) copy-start(s32[16]{0:T(128)} %counts_ref.5) | copy-start | bytes 196
  9.0 44.4 %collective-permute-start.1 = (bf16[4096,494]{0,1:T(8,128)(2,1)S(1)}, bf16[4096,494]{0,1:T(8,128)(2,1)S(1)}, u32[]{:S(2)}, u32[]{:S(2)}) collective-permute-start(bf16[4096,494]{0,1:T(8,128)(2,1)S(1)} %broadcast_select_fusion), channel_id=1, source_target_pairs={{0,1},{1,0},{2,3},{3,2},{4,5},{5,4},{6,7},{7,6},{8,9},{9,8},{10,11... | collective-permute-start | bytes 12140552 | tf_op jit(solution)/shard_map/ppermute | solution.py:172
  27.0 8.0 %collective-permute-start.8 = (bf16[128,512]{1,0:T(8,128)(2,1)S(1)}, bf16[128,512]{1,0:T(8,128)(2,1)S(1)}, u32[]{:S(2)}, u32[]{:S(2)}) collective-permute-start(bf16[128,512]{1,0:T(8,128)(2,1)S(1)} %get-tuple-element.59.refs_0_), channel_id=1, source_target_pairs={{0,2},{2,4},{4,6},{6,8},{8,10},{10,12},{12,14},{14,0},{1,3},{3,5},... | collective-permute-start | bytes 393224 | tf_op jit(solution)/shard_map/ppermute | solution.py:176
  28.7 6.3 %collective-permute-start.3 = (bf16[128,512]{1,0:T(8,128)(2,1)S(1)}, bf16[128,512]{1,0:T(8,128)(2,1)S(1)}, u32[]{:S(2)}, u32[]{:S(2)}) collective-permute-start(bf16[128,512]{1,0:T(8,128)(2,1)S(1)} %get-tuple-element.60.refs_1_), channel_id=1, source_target_pairs={{0,14},{2,0},{4,2},{6,4},{8,6},{10,8},{12,10},{14,12},{1,15},{3,1}... | collective-permute-start | bytes 393224 | tf_op jit(solution)/shard_map/ppermute | solution.py:176
  32.7 5.0 %collective-permute-start.2 = (bf16[128,512]{1,0:T(8,128)(2,1)S(1)}, bf16[128,512]{1,0:T(8,128)(2,1)S(1)}, u32[]{:S(2)}, u32[]{:S(2)}) collective-permute-start(bf16[128,512]{1,0:T(8,128)(2,1)S(1)} %get-tuple-element.59.refs_0_), channel_id=1, source_target_pairs={{0,14},{2,0},{4,2},{6,4},{8,6},{10,8},{12,10},{14,12},{1,15},{3,1}... | collective-permute-start | bytes 393224 | tf_op jit(solution)/shard_map/ppermute | solution.py:176
  34.1 5.7 %collective-permute-start.13 = (bf16[128,512]{1,0:T(8,128)(2,1)S(1)}, bf16[128,512]{1,0:T(8,128)(2,1)S(1)}, u32[]{:S(2)}, u32[]{:S(2)}) collective-permute-start(bf16[128,512]{1,0:T(8,128)(2,1)S(1)} %get-tuple-element.60.refs_1_), channel_id=1, source_target_pairs={{0,2},{2,4},{4,6},{6,8},{8,10},{10,12},{12,14},{14,0},{1,3},{3,5},... | collective-permute-start | bytes 393224 | tf_op jit(solution)/shard_map/ppermute | solution.py:176
  35.0 5.5 %collective-permute-start.9 = (bf16[128,512]{1,0:T(8,128)(2,1)S(1)}, bf16[128,512]{1,0:T(8,128)(2,1)S(1)}, u32[]{:S(2)}, u32[]{:S(2)}) collective-permute-start(bf16[128,512]{1,0:T(8,128)(2,1)S(1)} %collective-permute-done.8.refs_14_), channel_id=1, source_target_pairs={{0,2},{2,4},{4,6},{6,8},{8,10},{10,12},{12,14},{14,0},{1,3},{3,5},... | collective-permute-start | bytes 393224 | tf_op jit(solution)/shard_map/ppermute | solution.py:176
  35.0 5.5 %collective-permute-start.5 = (bf16[128,512]{1,0:T(8,128)(2,1)S(1)}, bf16[128,512]{1,0:T(8,128)(2,1)S(1)}, u32[]{:S(2)}, u32[]{:S(2)}) collective-permute-start(bf16[128,512]{1,0:T(8,128)(2,1)S(1)} %collective-permute-done.3.refs_3_), channel_id=1, source_target_pairs={{0,14},{2,0},{4,2},{6,4},{8,6},{10,8},{12,10},{14,12},{1,15},{3,1}... | collective-permute-start | bytes 393224 | tf_op jit(solution)/shard_map/ppermute | solution.py:176
  37.8 5.7 %collective-permute-start.4 = (bf16[128,512]{1,0:T(8,128)(2,1)S(1)}, bf16[128,512]{1,0:T(8,128)(2,1)S(1)}, u32[]{:S(2)}, u32[]{:S(2)}) collective-permute-start(bf16[128,512]{1,0:T(8,128)(2,1)S(1)} %collective-permute-done.2.refs_2_), channel_id=1, source_target_pairs={{0,14},{2,0},{4,2},{6,4},{8,6},{10,8},{12,10},{14,12},{1,15},{3,1}... | collective-permute-start | bytes 393224 | tf_op jit(solution)/shard_map/ppermute | solution.py:176
  39.8 5.3 %collective-permute-start.14 = (bf16[128,512]{1,0:T(8,128)(2,1)S(1)}, bf16[128,512]{1,0:T(8,128)(2,1)S(1)}, u32[]{:S(2)}, u32[]{:S(2)}) collective-permute-start(bf16[128,512]{1,0:T(8,128)(2,1)S(1)} %collective-permute-done.13.refs_15_), channel_id=1, source_target_pairs={{0,2},{2,4},{4,6},{6,8},{8,10},{10,12},{12,14},{14,0},{1,3},{3,5},... | collective-permute-start | bytes 393224 | tf_op jit(solution)/shard_map/ppermute | solution.py:176
  40.5 6.0 %collective-permute-start.10 = (bf16[128,512]{1,0:T(8,128)(2,1)S(1)}, bf16[128,512]{1,0:T(8,128)(2,1)S(1)}, u32[]{:S(2)}, u32[]{:S(2)}) collective-permute-start(bf16[128,512]{1,0:T(8,128)(2,1)S(1)} %collective-permute-done.9.refs_12_), channel_id=1, source_target_pairs={{0,2},{2,4},{4,6},{6,8},{8,10},{10,12},{12,14},{14,0},{1,3},{3,5},... | collective-permute-start | bytes 393224 | tf_op jit(solution)/shard_map/ppermute | solution.py:176
  40.5 6.0 %collective-permute-start.7 = (bf16[128,512]{1,0:T(8,128)(2,1)S(1)}, bf16[128,512]{1,0:T(8,128)(2,1)S(1)}, u32[]{:S(2)}, u32[]{:S(2)}) collective-permute-start(bf16[128,512]{1,0:T(8,128)(2,1)S(1)} %collective-permute-done.5.refs_5_), channel_id=1, source_target_pairs={{0,14},{2,0},{4,2},{6,4},{8,6},{10,8},{12,10},{14,12},{1,15},{3,1}... | collective-permute-start | bytes 393224 | tf_op jit(solution)/shard_map/ppermute | solution.py:176
  43.5 6.3 %collective-permute-start.6 = (bf16[128,512]{1,0:T(8,128)(2,1)S(1)}, bf16[128,512]{1,0:T(8,128)(2,1)S(1)}, u32[]{:S(2)}, u32[]{:S(2)}) collective-permute-start(bf16[128,512]{1,0:T(8,128)(2,1)S(1)} %collective-permute-done.4.refs_4_), channel_id=1, source_target_pairs={{0,14},{2,0},{4,2},{6,4},{8,6},{10,8},{12,10},{14,12},{1,15},{3,1}... | collective-permute-start | bytes 393224 | tf_op jit(solution)/shard_map/ppermute | solution.py:176
  45.1 6.7 %collective-permute-start.15 = (bf16[128,512]{1,0:T(8,128)(2,1)S(1)}, bf16[128,512]{1,0:T(8,128)(2,1)S(1)}, u32[]{:S(2)}, u32[]{:S(2)}) collective-permute-start(bf16[128,512]{1,0:T(8,128)(2,1)S(1)} %collective-permute-done.14.refs_13_), channel_id=1, source_target_pairs={{0,2},{2,4},{4,6},{6,8},{8,10},{10,12},{12,14},{14,0},{1,3},{3,5},... | collective-permute-start | bytes 393224 | tf_op jit(solution)/shard_map/ppermute | solution.py:176
  46.5 6.9 %collective-permute-start.11 = (bf16[128,512]{1,0:T(8,128)(2,1)S(1)}, bf16[128,512]{1,0:T(8,128)(2,1)S(1)}, u32[]{:S(2)}, u32[]{:S(2)}) collective-permute-start(bf16[128,512]{1,0:T(8,128)(2,1)S(1)} %collective-permute-done.10.refs_10_), channel_id=1, source_target_pairs={{0,2},{2,4},{4,6},{6,8},{8,10},{10,12},{12,14},{14,0},{1,3},{3,5},... | collective-permute-start | bytes 393224 | tf_op jit(solution)/shard_map/ppermute | solution.py:176
  46.6 6.9 %collective-permute-start.12 = (bf16[128,512]{1,0:T(8,128)(2,1)S(1)}, bf16[128,512]{1,0:T(8,128)(2,1)S(1)}, u32[]{:S(2)}, u32[]{:S(2)}) collective-permute-start(bf16[128,512]{1,0:T(8,128)(2,1)S(1)} %collective-permute-done.7.refs_7_), channel_id=1, source_target_pairs={{0,14},{2,0},{4,2},{6,4},{8,6},{10,8},{12,10},{14,12},{1,15},{3,1}... | collective-permute-start | bytes 393224 | tf_op jit(solution)/shard_map/ppermute | solution.py:176
  81.3 5.1 %collective-permute-start.19 = (f16[128,512]{1,0:T(8,128)(2,1)S(1)}, f16[128,512]{1,0:T(8,128)(2,1)S(1)}, u32[]{:S(2)}, u32[]{:S(2)}) collective-permute-start(f16[128,512]{1,0:T(8,128)(2,1)S(1)} %convert_element_type.98), channel_id=1, source_target_pairs={{0,2},{2,4},{4,6},{6,8},{8,10},{10,12},{12,14},{14,0},{1,3},{3,5},... | collective-permute-start | bytes 393224 | tf_op jit(solution)/shard_map/ppermute | solution.py:176
  81.7 4.8 %collective-permute-start.16 = (f16[128,512]{1,0:T(8,128)(2,1)S(1)}, f16[128,512]{1,0:T(8,128)(2,1)S(1)}, u32[]{:S(2)}, u32[]{:S(2)}) collective-permute-start(f16[128,512]{1,0:T(8,128)(2,1)S(1)} %convert_element_type.92), channel_id=1, source_target_pairs={{0,14},{2,0},{4,2},{6,4},{8,6},{10,8},{12,10},{14,12},{1,15},{3,1}... | collective-permute-start | bytes 393224 | tf_op jit(solution)/shard_map/ppermute | solution.py:176
  84.2 5.1 %collective-permute-start.26 = (f16[128,512]{1,0:T(8,128)(2,1)S(1)}, f16[128,512]{1,0:T(8,128)(2,1)S(1)}, u32[]{:S(2)}, u32[]{:S(2)}) collective-permute-start(f16[128,512]{1,0:T(8,128)(2,1)S(1)} %convert_element_type.112), channel_id=1, source_target_pairs={{0,14},{2,0},{4,2},{6,4},{8,6},{10,8},{12,10},{14,12},{1,15},{3,1}... | collective-permute-start | bytes 393224 | tf_op jit(solution)/shard_map/ppermute | solution.py:176
  84.3 6.4 %collective-permute-start.23 = (f16[128,512]{1,0:T(8,128)(2,1)S(1)}, f16[128,512]{1,0:T(8,128)(2,1)S(1)}, u32[]{:S(2)}, u32[]{:S(2)}) collective-permute-start(f16[128,512]{1,0:T(8,128)(2,1)S(1)} %convert_element_type.106), channel_id=1, source_target_pairs={{0,2},{2,4},{4,6},{6,8},{8,10},{10,12},{12,14},{14,0},{1,3},{3,5},... | collective-permute-start | bytes 393224 | tf_op jit(solution)/shard_map/ppermute | solution.py:176
  86.5 5.1 %collective-permute-start.20 = (f16[128,512]{1,0:T(8,128)(2,1)S(1)}, f16[128,512]{1,0:T(8,128)(2,1)S(1)}, u32[]{:S(2)}, u32[]{:S(2)}) collective-permute-start(f16[128,512]{1,0:T(8,128)(2,1)S(1)} %add_convert_fusion.7), channel_id=1, source_target_pairs={{0,2},{2,4},{4,6},{6,8},{8,10},{10,12},{12,14},{14,0},{1,3},{3,5},... | collective-permute-start | bytes 393224 | tf_op jit(solution)/shard_map/ppermute | solution.py:176
  86.6 5.1 %collective-permute-start.17 = (f16[128,512]{1,0:T(8,128)(2,1)S(1)}, f16[128,512]{1,0:T(8,128)(2,1)S(1)}, u32[]{:S(2)}, u32[]{:S(2)}) collective-permute-start(f16[128,512]{1,0:T(8,128)(2,1)S(1)} %add_convert_fusion.9), channel_id=1, source_target_pairs={{0,14},{2,0},{4,2},{6,4},{8,6},{10,8},{12,10},{14,12},{1,15},{3,1}... | collective-permute-start | bytes 393224 | tf_op jit(solution)/shard_map/ppermute | solution.py:176
  89.4 5.1 %collective-permute-start.27 = (f16[128,512]{1,0:T(8,128)(2,1)S(1)}, f16[128,512]{1,0:T(8,128)(2,1)S(1)}, u32[]{:S(2)}, u32[]{:S(2)}) collective-permute-start(f16[128,512]{1,0:T(8,128)(2,1)S(1)} %add_convert_fusion.2), channel_id=1, source_target_pairs={{0,14},{2,0},{4,2},{6,4},{8,6},{10,8},{12,10},{14,12},{1,15},{3,1}... | collective-permute-start | bytes 393224 | tf_op jit(solution)/shard_map/ppermute | solution.py:176
  90.8 5.6 %collective-permute-start.24 = (f16[128,512]{1,0:T(8,128)(2,1)S(1)}, f16[128,512]{1,0:T(8,128)(2,1)S(1)}, u32[]{:S(2)}, u32[]{:S(2)}) collective-permute-start(f16[128,512]{1,0:T(8,128)(2,1)S(1)} %add_convert_fusion.4), channel_id=1, source_target_pairs={{0,2},{2,4},{4,6},{6,8},{8,10},{10,12},{12,14},{14,0},{1,3},{3,5},... | collective-permute-start | bytes 393224 | tf_op jit(solution)/shard_map/ppermute | solution.py:176
  91.6 7.0 %collective-permute-start.21 = (f16[128,512]{1,0:T(8,128)(2,1)S(1)}, f16[128,512]{1,0:T(8,128)(2,1)S(1)}, u32[]{:S(2)}, u32[]{:S(2)}) collective-permute-start(f16[128,512]{1,0:T(8,128)(2,1)S(1)} %add_convert_fusion.6), channel_id=1, source_target_pairs={{0,2},{2,4},{4,6},{6,8},{8,10},{10,12},{12,14},{14,0},{1,3},{3,5},... | collective-permute-start | bytes 393224 | tf_op jit(solution)/shard_map/ppermute | solution.py:176
  91.8 10.5 %collective-permute-start.18 = (f16[128,512]{1,0:T(8,128)(2,1)S(1)}, f16[128,512]{1,0:T(8,128)(2,1)S(1)}, u32[]{:S(2)}, u32[]{:S(2)}) collective-permute-start(f16[128,512]{1,0:T(8,128)(2,1)S(1)} %add_convert_fusion.8), channel_id=1, source_target_pairs={{0,14},{2,0},{4,2},{6,4},{8,6},{10,8},{12,10},{14,12},{1,15},{3,1}... | collective-permute-start | bytes 393224 | tf_op jit(solution)/shard_map/ppermute | solution.py:176
  94.6 40.0 %copy-start.1 = (s32[8,64]{1,0:T(8,128)S(1)}, s32[8,64]{1,0:T(8,128)}, u32[]{:S(2)}) copy-start(s32[8,64]{1,0:T(8,128)} %get-tuple-element.52.places_ref) | copy-start | bytes 6148
  94.6 4.6 %collective-permute-start.28 = (f16[128,512]{1,0:T(8,128)(2,1)S(1)}, f16[128,512]{1,0:T(8,128)(2,1)S(1)}, u32[]{:S(2)}, u32[]{:S(2)}) collective-permute-start(f16[128,512]{1,0:T(8,128)(2,1)S(1)} %add_convert_fusion.1), channel_id=1, source_target_pairs={{0,14},{2,0},{4,2},{6,4},{8,6},{10,8},{12,10},{14,12},{1,15},{3,1}... | collective-permute-start | bytes 393224 | tf_op jit(solution)/shard_map/ppermute | solution.py:176
  96.4 7.9 %collective-permute-start.25 = (f16[128,512]{1,0:T(8,128)(2,1)S(1)}, f16[128,512]{1,0:T(8,128)(2,1)S(1)}, u32[]{:S(2)}, u32[]{:S(2)}) collective-permute-start(f16[128,512]{1,0:T(8,128)(2,1)S(1)} %add_convert_fusion.3), channel_id=1, source_target_pairs={{0,2},{2,4},{4,6},{6,8},{8,10},{10,12},{12,14},{14,0},{1,3},{3,5},... | collective-permute-start | bytes 393224 | tf_op jit(solution)/shard_map/ppermute | solution.py:176
  98.7 5.6 %collective-permute-start.22 = (f16[128,512]{1,0:T(8,128)(2,1)S(1)}, f16[128,512]{1,0:T(8,128)(2,1)S(1)}, u32[]{:S(2)}, u32[]{:S(2)}) collective-permute-start(f16[128,512]{1,0:T(8,128)(2,1)S(1)} %add_convert_fusion.5), channel_id=1, source_target_pairs={{0,2},{2,4},{4,6},{6,8},{8,10},{10,12},{12,14},{14,0},{1,3},{3,5},... | collective-permute-start | bytes 393224 | tf_op jit(solution)/shard_map/ppermute | solution.py:176
  99.2 5.9 %collective-permute-start.29 = (f16[128,512]{1,0:T(8,128)(2,1)S(1)}, f16[128,512]{1,0:T(8,128)(2,1)S(1)}, u32[]{:S(2)}, u32[]{:S(2)}) collective-permute-start(f16[128,512]{1,0:T(8,128)(2,1)S(1)} %add_convert_fusion), channel_id=1, source_target_pairs={{0,14},{2,0},{4,2},{6,4},{8,6},{10,8},{12,10},{14,12},{1,15},{3,1}... | collective-permute-start | bytes 393224 | tf_op jit(solution)/shard_map/ppermute | solution.py:176
  107.2 12.5 %all-to-all-start.2 = ((f16[16,32,512]{2,1,0:T(8,128)(2,1)}), f16[16,32,512]{2,1,0:T(8,128)(2,1)S(1)}, u32[]{:S(2)}, u32[]{:S(2)}) async-start(f16[16,32,512]{2,1,0:T(8,128)(2,1)} %bitcast.5), calls=%async_computation.2 | async-start | bytes 1048576 | tf_op jit(solution)/shard_map/all_to_all | solution.py:299
  119.9 14.7 %collective-permute-start.30 = (f32[32,256]{1,0:T(8,128)S(1)}, f32[32,256]{1,0:T(8,128)S(1)}, u32[]{:S(2)}, u32[]{:S(2)}) collective-permute-start(f32[32,256]{1,0:T(8,128)S(1)} %get-tuple-element.99), channel_id=1, source_target_pairs={{0,1},{1,0},{2,3},{3,2},{4,5},{5,4},{6,7},{7,6},{8,9},{9,8},{10,11... | collective-permute-start | bytes 98312 | tf_op jit(solution)/shard_map/ppermute | solution.py:172
